TPU v7x, 128 devices: a whole 4x4x4 slice. The times are simulated.
128 devices in a mesh: seq: 16 (over z, x), inter: 8 (over y, core).
Axes of the slice: x: 4, y: 4, z: 4, core: 2. Of those that a mesh axis runs over, the one named last changes fastest.
Arguments:
- queries: bfloat16 [2, 16, 512, 4096], P(None, 'seq', 'inter'), may hold values from -12 to 12
- span_keys: bfloat16 [2, 16, 512, 1024], P(None, 'seq', None, 'inter'), may hold values from -6 to 6
- span_values: bfloat16 [2, 16, 512, 1024], P(None, 'seq', None, 'inter'), may hold values from -6 to 6
- cache_keys: bfloat16 [32, 16, 512, 1024], P(None, 'seq', None, 'inter'), may hold values from -6 to 6
- cache_values: bfloat16 [32, 16, 512, 1024], P(None, 'seq', None, 'inter'), may hold values from -6 to 6
- block_key_scales: bfloat16 [32, 16, 8], P(None, 'seq', 'inter'), may hold values from 0.5 to 2
- value_scales: bfloat16 [32, 16, 8], P(None, 'seq', 'inter'), may hold values from 0.5 to 2
- selections: int32 [2, 16, 8, 3], P(None, 'seq', 'inter'), may hold values from 0 to 511, as said below
- start: int32 [1], replicated, may hold values from 253952 to 262144
Outputs:
- attended: bfloat16 [2, 16, 512, 4096], P(None, 'seq', 'inter')
Inputs may be any that keep to these rules, and one draw needn't show every extreme that they name: `selections`: cache block numbers. The three of one query block and group differ; the first lies in the last 16 blocks of the cache. For one group and one index s of seq, the 6 blocks selected by its query blocks have at most 2 on any one index b % 16, and exactly 2 on some.
All inputs are finite; a program needn't handle non-finite values.
Results may differ from a plain program's by a relative error of at most 0.0038.
Values may be sent and summed in bfloat16 or wider, within the bound.
A program may use at most 128 MiB of HBM per device.

v0:
```python
import math

import jax
import jax.numpy as jnp
from jax import lax
from jax.sharding import PartitionSpec as P

DH = 128
BLK = 512
HG = 4


def attend(
    query_vector,
    own_keys,
    own_values,
    chosen_keys,
    chosen_values,
    key_scale,
    value_scale,
    sel_blocks,
    cutoff,
    positions,
):
    row_count = query_vector.shape[0]
    head_count = query_vector.shape[1]
    head_dim = query_vector.shape[2]
    block_len = own_keys.shape[0]
    all_keys = jnp.concatenate([own_keys, chosen_keys.reshape(-1, head_dim)], axis=0)
    flat_query = query_vector.reshape(row_count * head_count, head_dim)
    scores = lax.dot_general(
        flat_query, all_keys, (((1,), (1,)), ((), ())), preferred_element_type=jnp.float32
    )
    column_scale = jnp.concatenate(
        [jnp.ones((block_len,), jnp.float32), jnp.repeat(key_scale.astype(jnp.float32), block_len)]
    )
    scores = scores * (column_scale / math.sqrt(head_dim))
    scores = scores.reshape(row_count, head_count, -1)
    key_index = jnp.arange(block_len, dtype=jnp.int32)
    own_ok = positions[:, None] >= key_index[None, :]
    sel_ok = (sel_blocks[:, None] * block_len + key_index[None, :] < cutoff).reshape(-1)
    allowed = jnp.concatenate(
        [own_ok, jnp.broadcast_to(sel_ok[None, :], (row_count, sel_ok.shape[0]))], axis=1
    )[:, None, :]
    top_score = jnp.max(jnp.where(allowed, scores, -jnp.inf), axis=-1, keepdims=True)
    weights = jnp.where(allowed, jnp.exp(jnp.where(allowed, scores, top_score) - top_score), 0.0)
    total = jnp.sum(weights, axis=-1, keepdims=True)
    rounded = weights.astype(jnp.bfloat16).reshape(row_count * head_count, -1)
    summed = jnp.dot(rounded[:, :block_len], own_values, preferred_element_type=jnp.float32)
    for index in range(chosen_values.shape[0]):
        piece = rounded[:, (index + 1) * block_len : (index + 2) * block_len]
        summed = summed + value_scale[index].astype(jnp.float32) * jnp.dot(
            piece, chosen_values[index], preferred_element_type=jnp.float32
        )
    return (summed.reshape(row_count, head_count, head_dim) / total).astype(jnp.bfloat16)


def per_device(
    queries,
    span_keys,
    span_values,
    cache_keys,
    cache_values,
    block_key_scales,
    value_scales,
    selections,
    start,
):
    blocks_here = queries.shape[0]
    groups_here = selections.shape[2]
    stored_blocks = cache_keys.shape[0]
    seq_count = lax.axis_size("seq")
    seq_rank = lax.axis_index("seq")
    item_count = 3 * blocks_here
    capacity = max(2, (item_count + seq_count - 1) // seq_count)
    cutoff = start[0]
    listed = lax.all_gather(selections, "seq", axis=1, tiled=True)
    wanted = jnp.transpose(listed, (1, 2, 0, 3)).reshape(seq_count, groups_here, item_count)
    owner_rank = wanted % seq_count
    local_row = wanted // seq_count
    is_mine = (owner_rank == seq_rank).astype(jnp.int32)
    ranking = jnp.cumsum(is_mine, axis=2) - 1
    slot_ids = jnp.arange(capacity, dtype=jnp.int32)
    slot_hits = (is_mine[..., None] == 1) & (ranking[..., None] == slot_ids)
    slot_block = jnp.sum(jnp.where(slot_hits, local_row[..., None], 0), axis=2)
    group_ids = jnp.arange(groups_here, dtype=jnp.int32)[None, :, None]
    stored_keys = cache_keys[:, 0].reshape(stored_blocks, BLK, groups_here, DH)
    stored_values = cache_values[:, 0].reshape(stored_blocks, BLK, groups_here, DH)
    picked_keys = stored_keys[slot_block, :, group_ids, :]
    picked_values = stored_values[slot_block, :, group_ids, :]
    packed = jnp.concatenate([picked_keys, picked_values], axis=-1)
    scale_pack = jnp.stack(
        [block_key_scales[:, 0][slot_block, group_ids], value_scales[:, 0][slot_block, group_ids]],
        axis=-1,
    )
    got_blocks, got_scales = (
        lax.all_to_all(packed, "seq", split_axis=0, concat_axis=0, tiled=True),
        lax.all_to_all(scale_pack, "seq", split_axis=0, concat_axis=0, tiled=True),
    )
    own_lists = jnp.transpose(selections[:, 0], (1, 0, 2)).reshape(groups_here, item_count)
    own_owner = own_lists % seq_count
    item_ids = jnp.arange(item_count, dtype=jnp.int32)
    earlier = (own_owner[:, :, None] == own_owner[:, None, :]) & (
        item_ids[None, None, :] < item_ids[None, :, None]
    )
    slot_of = jnp.sum(earlier.astype(jnp.int32), axis=2)
    group_rows = jnp.arange(groups_here, dtype=jnp.int32)[:, None]
    fetched_kv = got_blocks[own_owner, group_rows, slot_of]
    fetched_sc = got_scales[own_owner, group_rows, slot_of]
    inter_rank = lax.axis_index("inter")
    all_kv, all_sc = (
        lax.all_gather(fetched_kv, "inter", axis=0, tiled=True),
        lax.all_gather(fetched_sc, "inter", axis=0, tiled=True),
    )
    all_lists = lax.all_gather(selections, "inter", axis=2, tiled=True)
    whole_keys, whole_values = (
        lax.all_gather(span_keys, "inter", axis=3, tiled=True),
        lax.all_gather(span_values, "inter", axis=3, tiled=True),
    )
    group_total = all_kv.shape[0]
    row_count = queries.shape[2]
    positions = inter_rank * row_count + jnp.arange(row_count, dtype=jnp.int32)
    query_all = queries[:, 0].reshape(blocks_here, row_count, group_total, HG, DH)
    keys_all = whole_keys[:, 0].reshape(blocks_here, BLK, group_total, DH)
    values_all = whole_values[:, 0].reshape(blocks_here, BLK, group_total, DH)
    pack_all = jnp.transpose(
        all_kv.reshape(group_total, blocks_here, 3, BLK, 2 * DH), (1, 0, 2, 3, 4)
    )
    scale_all = jnp.transpose(all_sc.reshape(group_total, blocks_here, 3, 2), (1, 0, 2, 3))
    ids_all = all_lists[:, 0]

    def attend_block(inputs):
        query_vector, keys_one, values_one, pack_one, scale_one, ids_one = inputs

        def group_results(query_g, keys_g, values_g, pack_g, scale_g, ids_g):
            return attend(
                query_g,
                keys_g,
                values_g,
                pack_g[..., :DH],
                pack_g[..., DH:],
                scale_g[:, 0],
                scale_g[:, 1],
                ids_g,
                cutoff,
                positions,
            )

        return jax.vmap(group_results, in_axes=(1, 1, 1, 0, 0, 0), out_axes=1)(
            query_vector, keys_one, values_one, pack_one, scale_one, ids_one
        )

    result = lax.map(attend_block, (query_all, keys_all, values_all, pack_all, scale_all, ids_all))
    return result.reshape(blocks_here, 1, row_count, group_total * HG * DH)


def solution(mesh):
    placed = (
        P(None, "seq", "inter", None),
        P(None, "seq", None, "inter"),
        P(None, "seq", None, "inter"),
        P(None, "seq", None, "inter"),
        P(None, "seq", None, "inter"),
        P(None, "seq", "inter"),
        P(None, "seq", "inter"),
        P(None, "seq", "inter", None),
        P(),
    )
    return jax.shard_map(
        per_device,
        mesh=mesh,
        in_specs=placed,
        out_specs=P(None, "seq", "inter", None),
        check_vma=False,
    )
```

profile of v0, /device:TPU:1, one launch (start us, length us, event | category | flops | bytes accessed | tf_op | source)
XLA Modules:
  0.0 354.1 jit_solution(915612709523551935)
XLA Ops:
  6.5 18.5 %all_gather.20 = s32[2,16,1,3]{3,2,1,0:T(1,128)S(1)} all-gather(s32[2,1,1,3]{3,2,1,0:T(1,128)} %param.18), channel_id=1, replica_groups=mesh['seq'=16,'inter'=8] {'seq'}, dimensions={1}, use_global_device_ids=true | all-gather | bytes 408 | tf_op jit(solution)/shard_map/all_gather | solution.py:77
  25.4 5.2 %gather_fusion = bf16[32,512,128]{2,1,0:T(8,128)(2,1)} fusion(bf16[32,512,1,128]{3,1,0,2:T(8,128)(2,1)} %bitcast.143, s32[32]{0:T(128)S(1)} %reshape.502), kind=kCustom, calls=%fused_computation | custom fusion | bytes 8388864 | tf_op jit(solution)/shard_map/gather | solution.py:89
  30.6 5.2 %gather_fusion.1 = bf16[32,512,128]{2,1,0:T(8,128)(2,1)} fusion(bf16[32,512,1,128]{3,1,0,2:T(8,128)(2,1)} %bitcast.144, s32[32]{0:T(128)S(1)} %reshape.502), kind=kCustom, calls=%fused_computation.1 | custom fusion | bytes 8388864 | tf_op jit(solution)/shard_map/gather | solution.py:90
  35.9 7.7 %pad_maximum_fusion = bf16[16,1,2,512,256]{4,3,2,1,0:T(8,128)(2,1)} fusion(bf16[16,1,2,512,128]{4,3,2,1,0:T(8,128)(2,1)} %bitcast.137, bf16[16,1,2,512,128]{4,3,2,1,0:T(8,128)(2,1)} %bitcast.136), kind=kLoop, calls=%fused_computation.57 | loop fusion | flops 16777216 | bytes 16777216 | tf_op jit(solution)/shard_map/concatenate | solution.py:91
  43.6 4.9 %all-to-all-start = ((bf16[16,1,2,512,256]{4,3,2,1,0:T(8,128)(2,1)}), bf16[16,1,2,512,256]{4,3,2,1,0:T(8,128)(2,1)}, u32[]{:S(2)}, u32[]{:S(2)}) async-start(bf16[16,1,2,512,256]{4,3,2,1,0:T(8,128)(2,1)} %pad_maximum_fusion), calls=%async_computation | async-start | bytes 16777216 | tf_op jit(solution)/shard_map/all_to_all | solution.py:97
  52.2 107.6 %all-to-all-done = bf16[16,1,2,512,256]{4,3,2,1,0:T(8,128)(2,1)} async-done(((bf16[16,1,2,512,256]{4,3,2,1,0:T(8,128)(2,1)}), bf16[16,1,2,512,256]{4,3,2,1,0:T(8,128)(2,1)}, u32[]{:S(2)}, u32[]{:S(2)}) %all-to-all-start) | async-done | bytes 8388640 | tf_op jit(solution)/shard_map/all_to_all | solution.py:97
  159.8 5.2 %gather_fusion.2 = bf16[6,512,256]{2,1,0:T(8,128)(2,1)} fusion(bf16[16,1,2,512,256]{4,3,2,1,0:T(8,128)(2,1)} %all-to-all-done, s32[6]{0:T(128)S(1)} %or_bitcast_fusion), kind=kCustom, calls=%fused_computation.2 | custom fusion | bytes 3145800 | tf_op jit(solution)/shard_map/gather | solution.py:108
  167.4 5.2 %all-to-all-start.1 = ((bf16[16,1,2,2]{3,2,1,0:T(2,128)(2,1)}), bf16[16,1,2,2]{3,2,1,0:T(2,128)(2,1)S(1)}, u32[]{:S(2)}, u32[]{:S(2)}) async-start(bf16[16,1,2,2]{3,2,1,0:T(2,128)(2,1)} %pad_maximum_fusion.1), calls=%async_computation.1 | async-start | bytes 16384 | tf_op jit(solution)/shard_map/all_to_all | solution.py:98
  172.6 1.6 reshape_squeeze.15
  174.2 17.8 %all_gather.18 = s32[2,1,8,3]{3,0,1,2:T(2,128)S(1)} all-gather(s32[2,1,1,3]{3,0,1,2:T(2,128)S(1)} %bitcast.151), channel_id=1, replica_groups=mesh['seq'=16,'inter'=8] {'inter'}, dimensions={2}, use_global_device_ids=true | all-gather | bytes 216 | tf_op jit(solution)/shard_map/all_gather | solution.py:115
  192.8 8.2 %all-gather.2 = bf16[8,6,2]{1,2,0:T(2,128)(2,1)S(1)} all-gather(bf16[1,6,2]{1,2,0:T(2,128)(2,1)S(1)} %bitcast.152), channel_id=3, replica_groups=mesh['seq'=16,'inter'=8] {'inter'}, dimensions={0}, use_global_device_ids=true | all-gather | bytes 216 | tf_op jit(solution)/shard_map/all_gather | solution.py:113
  201.1 38.1 %all-gather.11.cloned.1.call-done = bf16[48,512,256]{2,1,0:T(8,128)(2,1)} async-done(((bf16[6,512,256]{2,1,0:T(8,128)(2,1)}), bf16[48,512,256]{2,1,0:T(8,128)(2,1)}) %all-gather.11.cloned.1.call-update) | async-done | bytes 12582928 | tf_op jit(solution)/shard_map/all_gather | solution.py:112
  239.2 105.7 %while.11 = (s32[]{:T(128)}, bf16[2,64,8,4,128]{4,3,2,1,0:T(4,128)(2,1)}, s32[2,8,3]{1,2,0:T(4,128)S(1)}, s32[]{:T(128)}, bf16[2,64,8,4,128]{4,3,2,1,0:T(4,128)(...) while((s32[]{:T(128)}, ...), condition=%wide.region_6.7_spmd.clone, body=%wide.region_3.6_spmd.clone.sunk | while | flops 2196836352 | bytes 167555056 | solution.py:153
  239.2 3.2 copy_bitcast_fusion.4
  243.1 2.5 copy.142
  247.5 4.8 %broadcast_in_dim.123 = pred[8,64,4,2048]{3,2,1,0:T(4,128)(4,1)} broadcast(pred[8,64,2048]{2,1,0:T(8,128)(4,1)S(1)} %pad_add_fusion.2), dimensions={0,1,3} | broadcast | bytes 5242880 | tf_op jit(solution)/shard_map/while/body/eval_jaxpr/vmap(jit(_where))/broadcast_in_dim | solution.py:46
  252.3 12.1 %broadcast_in_dim.124 = pred[8,256,2048]{2,1,0:T(32,128)(4,1)} reshape(pred[8,64,4,2048]{3,2,1,0:T(4,128)(4,1)} %broadcast_in_dim.123) | data formatting | bytes 8388608 | tf_op jit(solution)/shard_map/while/body/eval_jaxpr/vmap(jit(_where))/broadcast_in_dim | solution.py:46
  268.0 5.6 %select_reduce_fusion.2 = (f32[8,256]{1,0:T(8,128)S(1)}, f32[8,256,2048]{2,1,0:T(8,128)S(1)}) fusion(pred[8,256,2048]{2,1,0:T(32,128)(4,1)} %broadcast_in_dim.124, f32[8,2048]{1,0:T(8,128)S(1)} %pad_multiply_fusion.2, bf16[8,256,128]{2,1,0:T(8,128)(2,1)S(1)} %bitcast.134, bf16[8,1536,128]{2,1,0:T(8,128)(2,1)} %bitcast.131, ...), kind=kOutput, calls=%fused_computation.8.clone.1 | convolution fusion | flops 1094711296 | bytes 25763840 | tf_op jit(solution)/shard_map/while/body/eval_jaxpr/vmap()/dot_general | solution.py:31
  273.5 9.2 %fusion.78 = (f32[8,256]{1,0:T(8,128)S(1)}, bf16[8,256,2048]{2,1,0:T(8,128)(2,1)S(1)}) fusion(pred[8,256,2048]{2,1,0:T(32,128)(4,1)} %broadcast_in_dim.124, f32[8,256,2048]{2,1,0:T(8,128)S(1)} %get-tuple-element.237, f32[8,256]{1,0:T(8,128)S(1)} %get-tuple-element.238, f32[8,2048]{1,0:T(8,128)S(1)} %pad_multiply_fusion.2), kind=kLoop, calls=%fused_computation.9.clone.1 | loop fusion | flops 25163776 | bytes 29442048 | tf_op jit(solution)/shard_map/while/body/eval_jaxpr/vmap()/reduce_sum | solution.py:47
  282.8 1.9 fusion.79
  285.5 2.0 fusion.81
  287.5 1.9 fusion.82
  292.1 3.2 copy_bitcast_fusion.4
  295.9 2.5 copy.142
  300.4 4.8 %broadcast_in_dim.123 = pred[8,64,4,2048]{3,2,1,0:T(4,128)(4,1)} broadcast(pred[8,64,2048]{2,1,0:T(8,128)(4,1)S(1)} %pad_add_fusion.2), dimensions={0,1,3} | broadcast | bytes 5242880 | tf_op jit(solution)/shard_map/while/body/eval_jaxpr/vmap(jit(_where))/broadcast_in_dim | solution.py:46
  305.1 12.1 %broadcast_in_dim.124 = pred[8,256,2048]{2,1,0:T(32,128)(4,1)} reshape(pred[8,64,4,2048]{3,2,1,0:T(4,128)(4,1)} %broadcast_in_dim.123) | data formatting | bytes 8388608 | tf_op jit(solution)/shard_map/while/body/eval_jaxpr/vmap(jit(_where))/broadcast_in_dim | solution.py:46
  320.8 5.6 %select_reduce_fusion.2 = (f32[8,256]{1,0:T(8,128)S(1)}, f32[8,256,2048]{2,1,0:T(8,128)S(1)}) fusion(pred[8,256,2048]{2,1,0:T(32,128)(4,1)} %broadcast_in_dim.124, f32[8,2048]{1,0:T(8,128)S(1)} %pad_multiply_fusion.2, bf16[8,256,128]{2,1,0:T(8,128)(2,1)S(1)} %bitcast.134, bf16[8,1536,128]{2,1,0:T(8,128)(2,1)} %bitcast.131, ...), kind=kOutput, calls=%fused_computation.8.clone.1 | convolution fusion | flops 1094711296 | bytes 25763840 | tf_op jit(solution)/shard_map/while/body/eval_jaxpr/vmap()/dot_general | solution.py:31
  326.4 9.2 %fusion.78 = (f32[8,256]{1,0:T(8,128)S(1)}, bf16[8,256,2048]{2,1,0:T(8,128)(2,1)S(1)}) fusion(pred[8,256,2048]{2,1,0:T(32,128)(4,1)} %broadcast_in_dim.124, f32[8,256,2048]{2,1,0:T(8,128)S(1)} %get-tuple-element.237, f32[8,256]{1,0:T(8,128)S(1)} %get-tuple-element.238, f32[8,2048]{1,0:T(8,128)S(1)} %pad_multiply_fusion.2), kind=kLoop, calls=%fused_computation.9.clone.1 | loop fusion | flops 25163776 | bytes 29442048 | tf_op jit(solution)/shard_map/while/body/eval_jaxpr/vmap()/reduce_sum | solution.py:47
  335.7 1.9 fusion.79
  338.3 2.0 fusion.81
  340.4 1.9 fusion.82
  344.9 2.6 reshape.495
  (124 shorter events, 25.9 us)
Async XLA Ops:
  6.5 158.5 %copy-start = (bf16[32,1,1]{0,2,1:T(2,128)(2,1)S(1)}, bf16[32,1,1]{0,2,1:T(2,128)(2,1)}, u32[]{:S(2)}) copy-start(bf16[32,1,1]{0,2,1:T(2,128)(2,1)} %param.16) | copy-start | bytes 196
  43.6 5.0 %copy-start.8 = (bf16[2,1,512,128]{3,2,1,0:T(8,128)(2,1)S(1)}, bf16[2,1,512,128]{3,2,1,0:T(8,128)(2,1)}, u32[]{:S(2)}) copy-start(bf16[2,1,512,128]{3,2,1,0:T(8,128)(2,1)} %param.13) | copy-start | bytes 786436
  43.6 5.9 %copy-start.9 = (bf16[2,1,512,128]{3,2,1,0:T(8,128)(2,1)S(1)}, bf16[2,1,512,128]{3,2,1,0:T(8,128)(2,1)}, u32[]{:S(2)}) copy-start(bf16[2,1,512,128]{3,2,1,0:T(8,128)(2,1)} %param.12) | copy-start | bytes 786436
  43.6 7.4 %copy-start.10 = (s32[2,1,1,3]{3,2,1,0:T(1,128)S(1)}, s32[2,1,1,3]{3,2,1,0:T(1,128)}, u32[]{:S(2)}) copy-start(s32[2,1,1,3]{3,2,1,0:T(1,128)} %param.18) | copy-start | bytes 76
  43.6 116.2 %all-to-all-start = ((bf16[16,1,2,512,256]{4,3,2,1,0:T(8,128)(2,1)}), bf16[16,1,2,512,256]{4,3,2,1,0:T(8,128)(2,1)}, u32[]{:S(2)}, u32[]{:S(2)}) async-start(bf16[16,1,2,512,256]{4,3,2,1,0:T(8,128)(2,1)} %pad_maximum_fusion), calls=%async_computation | async-start | bytes 16777216 | tf_op jit(solution)/shard_map/all_to_all | solution.py:97
  48.5 117.4 %copy-start.2 = (bf16[32,1,1]{0,2,1:T(2,128)(2,1)S(1)}, bf16[32,1,1]{0,2,1:T(2,128)(2,1)}, u32[]{:S(2)}) copy-start(bf16[32,1,1]{0,2,1:T(2,128)(2,1)} %param.17) | copy-start | bytes 196
  48.5 152.6 %all-gather.9.cloned.1.call-start = ((), (), s32[]{:S(2)}) async-start(), calls=%async_computation.3 | async-start | bytes 2359296 | tf_op jit(solution)/shard_map/all_gather | solution.py:118
  49.5 151.6 %all-gather.7.cloned.1.call-start = ((), (), s32[]{:S(2)}) async-start(), calls=%async_computation.2 | async-start | bytes 2359296 | tf_op jit(solution)/shard_map/all_gather | solution.py:117
  50.4 188.8 %all-gather.11.cloned.1.call-start = ((), (), s32[]{:S(2)}) async-start(), calls=%async_computation.4 | async-start | bytes 14155776 | tf_op jit(solution)/shard_map/all_gather | solution.py:112
  52.2 120.5 %copy-start.5 = (bf16[2,1,64,4096]{3,2,1,0:T(8,128)(2,1)S(1)}, bf16[2,1,64,4096]{3,2,1,0:T(8,128)(2,1)}, u32[]{:S(2)}) copy-start(bf16[2,1,64,4096]{3,2,1,0:T(8,128)(2,1)} %param.11) | copy-start | bytes 3145732
  167.4 24.6 %all-to-all-start.1 = ((bf16[16,1,2,2]{3,2,1,0:T(2,128)(2,1)}), bf16[16,1,2,2]{3,2,1,0:T(2,128)(2,1)S(1)}, u32[]{:S(2)}, u32[]{:S(2)}) async-start(bf16[16,1,2,2]{3,2,1,0:T(2,128)(2,1)} %pad_maximum_fusion.1), calls=%async_computation.1 | async-start | bytes 16384 | tf_op jit(solution)/shard_map/all_to_all | solution.py:98
  242.5 3.8 %copy-start.3 = (bf16[8,3,512,256]{3,2,0,1:T(8,128)(2,1)}, bf16[8,3,512,256]{3,2,0,1:T(8,128)(2,1)S(1)}, u32[]{:S(2)}) copy-start(bf16[8,3,512,256]{3,2,0,1:T(8,128)(2,1)S(1)} %copy_bitcast_fusion.4) | copy-start | bytes 18874372 | tf_op jit(solution)/shard_map/while
  273.5 11.2 %copy-start.4 = (bf16[2,512,8,128]{1,3,2,0:T(8,128)(2,1)S(1)}, bf16[2,512,8,128]{1,3,2,0:T(8,128)(2,1)}, u32[]{:S(2)}) copy-start(bf16[2,512,8,128]{1,3,2,0:T(8,128)(2,1)} %get-tuple-element.275) | copy-start | bytes 6291460 | tf_op jit(solution)/shard_map/while
  285.5 4.6 %copy-start.6 = (bf16[2,64,8,4,128]{4,3,2,1,0:T(4,128)(2,1)S(1)}, bf16[2,64,8,4,128]{4,3,2,1,0:T(4,128)(2,1)}, u32[]{:S(2)}) copy-start(bf16[2,64,8,4,128]{4,3,2,1,0:T(4,128)(2,1)} %get-tuple-element.257) | copy-start | bytes 3145732 | tf_op jit(solution)/shard_map/while
  291.1 1.0 copy-start.7
  295.3 3.8 %copy-start.3 = (bf16[8,3,512,256]{3,2,0,1:T(8,128)(2,1)}, bf16[8,3,512,256]{3,2,0,1:T(8,128)(2,1)S(1)}, u32[]{:S(2)}) copy-start(bf16[8,3,512,256]{3,2,0,1:T(8,128)(2,1)S(1)} %copy_bitcast_fusion.4) | copy-start | bytes 18874372 | tf_op jit(solution)/shard_map/while
  326.4 11.2 %copy-start.4 = (bf16[2,512,8,128]{1,3,2,0:T(8,128)(2,1)S(1)}, bf16[2,512,8,128]{1,3,2,0:T(8,128)(2,1)}, u32[]{:S(2)}) copy-start(bf16[2,512,8,128]{1,3,2,0:T(8,128)(2,1)} %get-tuple-element.275) | copy-start | bytes 6291460 | tf_op jit(solution)/shard_map/while
  338.3 4.6 %copy-start.6 = (bf16[2,64,8,4,128]{4,3,2,1,0:T(4,128)(2,1)S(1)}, bf16[2,64,8,4,128]{4,3,2,1,0:T(4,128)(2,1)}, u32[]{:S(2)}) copy-start(bf16[2,64,8,4,128]{4,3,2,1,0:T(4,128)(2,1)} %get-tuple-element.257) | copy-start | bytes 3145732 | tf_op jit(solution)/shard_map/while
  343.9 1.0 copy-start.7
  344.9 2.6 copy-start.1
Sparse Core Ops, SparseCore 0:
  51.1 32.3 all-gather.8
  85.1 25.4 all-gather.6
  165.2 74.0 all-gather.10
where the time goes:
time: 356 us; the launch traced here: 354 us
  waiting for transfers between devices  146 us (41%)
  local copies, waits for them, and re-layouts  83.7 us (24%)
  blocking collectives  44.5 us (12%)
  other arithmetic  31.8 us (9%)
  matrix products  24.4 us (7%)
  between operations  13.3 us (4%)
  starting transfers between devices  10.2 us (3%)
    all_to_all x1, waiting for transfers between devices, per_device(): lax.all_to_all(packed, 'seq', split_axis=0, concat_axis=0, tiled=True)  108 us
    all_gather x1, waiting for transfers between devices, per_device(): lax.all_gather(fetched_kv, 'inter', axis=0, tiled=True)  38.1 us
    broadcast_in_dim x4, local copies, waits for them, and re-layouts, attend(): jnp.where(allowed, jnp.exp(jnp.where(allowed, scores, top_score) - top_sc...  33.8 us
    all_gather x1, blocking collectives, per_device(): listed = lax.all_gather(selections, 'seq', axis=1, tiled=True)  18.5 us
    reduce_sum x2, other arithmetic, attend(): total = jnp.sum(weights, axis=-1, keepdims=True)  18.5 us
    all_gather x1, blocking collectives, per_device(): all_lists = lax.all_gather(selections, 'inter', axis=2, tiled=True)  17.8 us
    dot_general x6, matrix products, attend(): jnp.dot(piece, chosen_values[index], preferred_element_type=jnp.float32)  11.7 us
    dot_general x2, matrix products, attend(): lax.dot_general(flat_query, all_keys, (((1,), (1,)), ((), ())), preferred...  11.1 us
  transfers between devices with their start and end apart: 5, of which 2 were waited for; matrix products, arithmetic and copies ran while one was open for 4% of the time, Pallas kernels for 0%

commit v1 on v0

--- a/solution.py
+++ b/solution.py
@@ -1,13 +1,31 @@
+import functools
 import math
 
 import jax
 import jax.numpy as jnp
+import numpy as np
 from jax import lax
+from jax.experimental import pallas as pl
+from jax.experimental.pallas import tpu as pltpu
 from jax.sharding import PartitionSpec as P
 
 DH = 128
 BLK = 512
 HG = 4
+SIDE = 4
+NODES = SIDE * SIDE
+ROWS_KV = 32
+SLOTS = 7
+SLOTS_FIRST = 6
+CANDS = 8
+PEERS = 8
+QROWS = BLK // PEERS
+WIDE = HG * DH
+TILE_ROWS = HG * QROWS
+POOL = ROWS_KV + 4 * SLOTS
+LOG2E = 1.4426950408889634
+NEG = -1e30
+MESH = pl.DeviceIdType.MESH
 
 
 def attend(
@@ -55,7 +73,7 @@
     return (summed.reshape(row_count, head_count, head_dim) / total).astype(jnp.bfloat16)
 
 
-def per_device(
+def exchange_all(
     queries,
     span_keys,
     span_values,
@@ -154,6 +172,465 @@
     return result.reshape(blocks_here, 1, row_count, group_total * HG * DH)
 
 
+def path_tables():
+    def move(node, way):
+        z, x = divmod(node, SIDE)
+        dz, dx = ((0, 1), (0, -1), (1, 0), (-1, 0))[way]
+        return (z + dz) % SIDE * SIDE + (x + dx) % SIDE
+
+    def paths(here, there):
+        if here == there:
+            return [[]]
+        z, x = divmod(here, SIDE)
+        tz, tx = divmod(there, SIDE)
+        rx, rz = (tx - x) % SIDE, (tz - z) % SIDE
+        ways = [w for w, ok in enumerate((rx in (1, 2), rx in (2, 3), rz in (1, 2), rz in (2, 3))) if ok]
+        return [[here * 4 + w] + rest for w in ways for rest in paths(move(here, w), there)]
+
+    table = np.zeros((NODES * NODES, CANDS, 4), np.int32)
+    dist = np.zeros((NODES * NODES,), np.int32)
+    for owner in range(NODES):
+        for dest in range(NODES):
+            found = paths(owner, dest)
+            pair = owner * NODES + dest
+            dist[pair] = len(found[0])
+            count = min(CANDS, len(found))
+            for c in range(count):
+                path = found[c * len(found) // count]
+                table[pair, c, : len(path)] = path
+    slot_of = np.zeros((256,), np.int32)
+    for bit in range(8):
+        slot_of[1 << bit] = bit
+    return np.concatenate([table.reshape(-1), dist, slot_of])
+
+
+TABLES = path_tables()
+DIST_AT = NODES * NODES * CANDS * 4
+SLOT_AT = DIST_AT + NODES * NODES
+CHOICES = {4: CANDS, 3: 6, 2: 2, 1: 1}
+
+
+def lists_kernel(x_ref, f_ref, i_ref, buf, send_sem, recv_sem):
+    s, r = lax.axis_index("seq"), lax.axis_index("inter")
+    barrier = pltpu.get_barrier_semaphore()
+    for k in range(1, NODES):
+        pl.semaphore_signal(
+            barrier, inc=1, device_id=(lax.rem(s + k, NODES), r), device_id_type=MESH
+        )
+    pl.semaphore_wait(barrier, NODES - 1)
+    copies = []
+    for k in range(1, NODES):
+        copy = pltpu.make_async_remote_copy(
+            src_ref=x_ref,
+            dst_ref=buf.at[s],
+            send_sem=send_sem.at[k],
+            recv_sem=recv_sem.at[k],
+            device_id=(lax.rem(s + k, NODES), r),
+            device_id_type=MESH,
+        )
+        copy.start()
+        copies.append(copy)
+    buf[s] = x_ref[...]
+    for copy in copies:
+        copy.wait()
+    got = buf[...]
+    f_ref[...] = got
+    i_ref[...] = got.astype(jnp.int32)
+
+
+def plan_kernel(
+    lists, scales, start, tab, send, place, limit, factor, flag, occ, bucket, cnt, tbl, posn
+):
+    me = lax.axis_index("seq")
+
+    def clear(i, _):
+        occ[i] = 0
+        return 0
+
+    lax.fori_loop(0, NODES * 4, clear, 0, unroll=8)
+    for i in range(9):
+        cnt[i] = 0
+    for t in range(SLOTS):
+        for d in range(4):
+            tbl[(me * 4 + d) * 8 + t] = 0
+
+    def sort_dest(dest, _):
+        for jk in range(6):
+            block = lists[dest, 0, 64 + jk]
+            owner = block & (NODES - 1)
+            steps = tab[DIST_AT + owner * NODES + dest]
+            posn[dest * 8 + jk] = block >> 4
+            kind = jnp.where(steps == 0, 8, (jk // 3) * 4 + 4 - steps)
+            at = cnt[kind]
+            bucket[kind * 48 + at] = dest * 8 + jk
+            cnt[kind] = at + 1
+        return 0
+
+    lax.fori_loop(0, NODES, sort_dest, 0)
+
+    def chain(base, hops):
+        links, marks = [], []
+        seen = None
+        for h in range(hops):
+            link = tab[base + h]
+            used = occ[link]
+            if seen is not None:
+                used = used | seen
+            mark = (~used) & (used + 1)
+            seen = mark | (mark - 1)
+            links.append(link)
+            marks.append(mark)
+        return links, marks
+
+    over = jnp.int32(0)
+    for j in range(2):
+        bound = 1 << (SLOTS_FIRST if j == 0 else SLOTS)
+        for hops in (4, 3, 2, 1):
+            kind = j * 4 + 4 - hops
+
+            def route(i, over, kind=kind, hops=hops, bound=bound):
+                item = bucket[kind * 48 + i]
+                dest = item >> 3
+                block = lists[dest, 0, 64 + (item & 7)]
+                owner = block & (NODES - 1)
+                base = (owner * NODES + dest) * (CANDS * 4)
+                best_at, best = base, None
+                for c in range(CHOICES[hops]):
+                    cost = chain(base + 4 * c, hops)[1][-1]
+                    if best is None:
+                        best = cost
+                    else:
+                        best_at = jnp.where(cost < best, base + 4 * c, best_at)
+                        best = jnp.minimum(cost, best)
+                fits = best < bound
+
+                @pl.when(fits)
+                def _():
+                    links, marks = chain(best_at, hops)
+                    source = block >> 4
+                    for link, mark in zip(links, marks):
+                        occ[link] = occ[link] | mark
+                        slot = tab[SLOT_AT + mark]
+                        tbl[link * 8 + slot] = source
+                        source = ROWS_KV + 4 * slot + (link & 3)
+                    posn[item] = source
+
+                return over | jnp.where(fits, 0, 1)
+
+            over = lax.fori_loop(0, cnt[kind], route, over)
+
+    for t in range(SLOTS):
+        for d in range(4):
+            send[t * 4 + d] = tbl[(me * 4 + d) * 8 + t]
+    for jk in range(6):
+        block = lists[me, 0, 64 + jk]
+        owner = block & (NODES - 1)
+        row = block >> 4
+        place[jk] = posn[me * 8 + jk]
+        limit[jk] = start[0] - block * BLK
+        factor[jk] = scales[owner, 0, row] * (LOG2E / math.sqrt(DH))
+        factor[8 + jk] = scales[owner, 0, ROWS_KV + row]
+    flag[...] = jnp.full((1, 128), over, jnp.int32).astype(jnp.float32)
+
+
+def main_kernel(
+    send, place, limit, factor, flag, q, sk_hbm, sv_hbm, ck_hbm, cv_hbm,
+    out, over,
+    kp, vp, snd, rcv, qb, ob, sk, sv, acc, top, flags,
+    load_sem, kv_send, kv_recv, q_send, q_recv, o_send, o_recv, f_send, f_recv,
+):
+    s, r = lax.axis_index("seq"), lax.axis_index("inter")
+    z, x = s // SIDE, s % SIDE
+    y, core = r // 2, r % 2
+    beside = (
+        z * SIDE + (x + 1) % SIDE,
+        z * SIDE + (x + 3) % SIDE,
+        (z + 1) % SIDE * SIDE + x,
+        (z + 3) % SIDE * SIDE + x,
+    )
+
+    def peer(k):
+        pair = k // 2
+        dy = (2 + 3 * pair + 3 * (pair * (pair - 1) // 2)) % 4
+        return (y + dy) % 4 * 2 + (core + 1 + k) % 2
+
+    loads = [
+        pltpu.make_async_copy(ck_hbm.at[:, 0], kp.at[pl.ds(0, ROWS_KV)], load_sem.at[0]),
+        pltpu.make_async_copy(cv_hbm.at[:, 0], vp.at[pl.ds(0, ROWS_KV)], load_sem.at[1]),
+        pltpu.make_async_copy(sk_hbm.at[:, 0], sk, load_sem.at[2]),
+        pltpu.make_async_copy(sv_hbm.at[:, 0], sv, load_sem.at[3]),
+        pltpu.make_async_copy(
+            q.at[:, 0, :, pl.ds(pl.multiple_of(r * WIDE, WIDE), WIDE)],
+            qb.at[:, pl.ds(pl.multiple_of(r * QROWS, QROWS), QROWS)],
+            load_sem.at[4],
+        ),
+    ]
+    for load in loads:
+        load.start()
+
+    barrier = pltpu.get_barrier_semaphore()
+    for n in beside:
+        pl.semaphore_signal(barrier, inc=1, device_id=(n, r), device_id_type=MESH)
+    for k in range(PEERS - 1):
+        pl.semaphore_signal(barrier, inc=1, device_id=(s, peer(k)), device_id_type=MESH)
+    pl.semaphore_wait(barrier, PEERS + 3)
+
+    def kv_copy(t, d, h):
+        return pltpu.make_async_remote_copy(
+            src_ref=snd.at[t, d, h],
+            dst_ref=rcv.at[t, d, h],
+            send_sem=kv_send.at[t, d, h],
+            recv_sem=kv_recv.at[t, d, h],
+            device_id=(beside[d], r),
+            device_id_type=MESH,
+        )
+
+    def q_copy(k):
+        to = peer(k)
+        return pltpu.make_async_remote_copy(
+            src_ref=q.at[:, 0, :, pl.ds(pl.multiple_of(to * WIDE, WIDE), WIDE)],
+            dst_ref=qb.at[:, pl.ds(pl.multiple_of(r * QROWS, QROWS), QROWS)],
+            send_sem=q_send.at[k],
+            recv_sem=q_recv.at[k],
+            device_id=(s, to),
+            device_id_type=MESH,
+        )
+
+    def f_copy(k):
+        return pltpu.make_async_remote_copy(
+            src_ref=flag,
+            dst_ref=flags.at[r],
+            send_sem=f_send.at[k],
+            recv_sem=f_recv.at[k],
+            device_id=(s, peer(k)),
+            device_id_type=MESH,
+        )
+
+    def o_copy(j, k):
+        to = peer(k)
+        return pltpu.make_async_remote_copy(
+            src_ref=ob.at[j, pl.ds(pl.multiple_of(to * QROWS, QROWS), QROWS)],
+            dst_ref=out.at[j, 0, :, pl.ds(pl.multiple_of(r * WIDE, WIDE), WIDE)],
+            send_sem=o_send.at[j, k],
+            recv_sem=o_recv.at[j, k],
+            device_id=(s, to),
+            device_id_type=MESH,
+        )
+
+    def o_own(j):
+        return pltpu.make_async_copy(
+            ob.at[j, pl.ds(pl.multiple_of(r * QROWS, QROWS), QROWS)],
+            out.at[j, 0, :, pl.ds(pl.multiple_of(r * WIDE, WIDE), WIDE)],
+            load_sem.at[5 + j],
+        )
+
+    def pump(t, h):
+        pool = (kp, vp)[h]
+        if t > 0:
+            for d in range(4):
+                kv_copy(t - 1, d, h).wait_recv()
+            for d in range(4):
+                pool[ROWS_KV + 4 * (t - 1) + d] = rcv[t - 1, d, h]
+        if t < SLOTS:
+            for d in range(4):
+                snd[t, d, h] = pool[send[t * 4 + d]]
+                kv_copy(t, d, h).start()
+
+    def rows_of(c):
+        return pl.ds(pl.multiple_of(c * QROWS, QROWS), QROWS)
+
+    def load_q(j, c):
+        tile = qb[j, rows_of(c), :]
+        return jnp.concatenate([tile[:, h * DH : (h + 1) * DH] for h in range(HG)], axis=0)
+
+    def scores_of(query, keys):
+        return lax.dot_general(
+            query, keys, (((1,), (1,)), ((), ())), preferred_element_type=jnp.float32
+        )
+
+    ones = jnp.ones((BLK, DH), jnp.bfloat16)
+    column = lax.broadcasted_iota(jnp.int32, (1, BLK), 1)
+
+    def own_tile(j, c):
+        scores = scores_of(load_q(j, c), sk[j]) * (LOG2E / math.sqrt(DH))
+        row = lax.broadcasted_iota(jnp.int32, (TILE_ROWS, 1), 0) % QROWS + c * QROWS
+        scores = jnp.where(column <= row, scores, NEG)
+        high = jnp.max(scores, axis=1, keepdims=True)
+        weights = jnp.exp2(scores - high).astype(jnp.bfloat16)
+        acc[j, c] = jnp.dot(
+            weights, jnp.concatenate([sv[j], ones], axis=1), preferred_element_type=jnp.float32
+        )
+        top[j, c] = jnp.broadcast_to(high, (TILE_ROWS, DH))
+
+    def cache_tile(j, c):
+        query = load_q(j, c)
+        before = top[j, c][:, :1]
+        parts = []
+        high = before
+        for i in range(3 * j, 3 * j + 3):
+            bias = jnp.where(column < limit[i], 0.0, NEG)
+            part = scores_of(query, kp[place[i]]) * factor[i] + bias
+            high = jnp.maximum(high, jnp.max(part, axis=1, keepdims=True))
+            parts.append(part)
+        fade = jnp.exp2(before - high)
+        old = acc[j, c]
+        summed = old[:, :DH] * fade
+        total = old[:, DH:] * fade
+        for i, part in zip(range(3 * j, 3 * j + 3), parts):
+            weights = jnp.exp2(part - high).astype(jnp.bfloat16)
+            more = jnp.dot(
+                weights,
+                jnp.concatenate([vp[place[i]], ones], axis=1),
+                preferred_element_type=jnp.float32,
+            )
+            summed = summed + more[:, :DH] * factor[8 + i]
+            total = total + more[:, DH:]
+        done = (summed / total).astype(jnp.bfloat16)
+        for h in range(HG):
+            ob[j, rows_of(c), h * DH : (h + 1) * DH] = done[h * QROWS : (h + 1) * QROWS]
+
+    def own_block(j):
+        def step(c, _):
+            own_tile(j, c)
+            return 0
+
+        lax.fori_loop(0, PEERS, step, 0)
+
+    def cache_blocks(j):
+        def step(k, _):
+            cache_tile(j, peer(k))
+            o_copy(j, k).start()
+            return 0
+
+        lax.fori_loop(0, PEERS - 1, step, 0)
+        cache_tile(j, r)
+        o_own(j).start()
+
+    for k in range(PEERS - 1):
+        q_copy(k).start()
+    loads[0].wait()
+    pump(0, 0)
+    loads[1].wait()
+    pump(0, 1)
+    for k in range(PEERS - 1):
+        f_copy(k).start()
+    flags[r] = flag[...]
+    for load in loads[2:]:
+        load.wait()
+    for t in range(1, SLOTS + 1):
+        for h in range(2):
+            pump(t, h)
+            if (t, h) == (3, 0):
+                for k in range(PEERS - 1):
+                    q_copy(k).wait()
+                own_block(0)
+            if (t, h) == (4, 0):
+                own_block(1)
+            if (t, h) == (SLOTS_FIRST, 1):
+                cache_blocks(0)
+    cache_blocks(1)
+    for k in range(PEERS - 1):
+        f_copy(k).wait()
+    worst = flags[0]
+    for k in range(1, PEERS):
+        worst = jnp.maximum(worst, flags[k])
+    over[...] = worst
+    for t in range(SLOTS):
+        for d in range(4):
+            for h in range(2):
+                kv_copy(t, d, h).wait_send()
+    for j in range(2):
+        o_own(j).wait()
+        for k in range(PEERS - 1):
+            o_copy(j, k).wait()
+
+
+def routed(
+    queries, span_keys, span_values, cache_keys, cache_values, key_scales, value_scales, selections, start
+):
+    f32, i32, bf16 = jnp.float32, jnp.int32, jnp.bfloat16
+    smem = pl.BlockSpec(memory_space=pltpu.SMEM)
+    vmem = pl.BlockSpec(memory_space=pltpu.VMEM)
+    hbm = pl.BlockSpec(memory_space=pl.ANY)
+    dma = pltpu.SemaphoreType.DMA
+    row = jnp.concatenate(
+        [key_scales.reshape(-1).astype(f32), value_scales.reshape(-1).astype(f32), selections.reshape(-1).astype(f32)]
+    )
+    row = jnp.pad(row, (0, 128 - row.shape[0])).reshape(1, 128)
+    scales, lists = pl.pallas_call(
+        lists_kernel,
+        out_shape=(
+            jax.ShapeDtypeStruct((NODES, 1, 128), f32),
+            jax.ShapeDtypeStruct((NODES, 1, 128), i32),
+        ),
+        in_specs=[vmem],
+        out_specs=(vmem, vmem),
+        scratch_shapes=[pltpu.VMEM((NODES, 1, 128), f32), dma((NODES,)), dma((NODES,))],
+        compiler_params=pltpu.CompilerParams(collective_id=0, has_side_effects=True),
+        name="lists",
+    )(row)
+    send, place, limit, factor, flag = pl.pallas_call(
+        plan_kernel,
+        out_shape=(
+            jax.ShapeDtypeStruct((4 * SLOTS,), i32),
+            jax.ShapeDtypeStruct((8,), i32),
+            jax.ShapeDtypeStruct((8,), i32),
+            jax.ShapeDtypeStruct((16,), f32),
+            jax.ShapeDtypeStruct((1, 128), f32),
+        ),
+        in_specs=[smem] * 4,
+        out_specs=(smem, smem, smem, smem, vmem),
+        scratch_shapes=[
+            pltpu.SMEM((NODES * 4,), i32),
+            pltpu.SMEM((9 * 48 + 96,), i32),
+            pltpu.SMEM((16,), i32),
+            pltpu.SMEM((NODES * 4 * 8,), i32),
+            pltpu.SMEM((NODES * 8,), i32),
+        ],
+        name="plan",
+    )(lists, scales, start, jnp.asarray(TABLES))
+    return pl.pallas_call(
+        main_kernel,
+        out_shape=(
+            jax.ShapeDtypeStruct(queries.shape, bf16),
+            jax.ShapeDtypeStruct((1, 128), f32),
+        ),
+        in_specs=[smem] * 4 + [vmem] + [hbm] * 5,
+        out_specs=(hbm, vmem),
+        scratch_shapes=[
+            pltpu.VMEM((POOL, BLK, DH), bf16),
+            pltpu.VMEM((POOL, BLK, DH), bf16),
+            pltpu.VMEM((SLOTS, 4, 2, BLK, DH), bf16),
+            pltpu.VMEM((SLOTS, 4, 2, BLK, DH), bf16),
+            pltpu.VMEM((2, BLK, WIDE), bf16),
+            pltpu.VMEM((2, BLK, WIDE), bf16),
+            pltpu.VMEM((2, BLK, DH), bf16),
+            pltpu.VMEM((2, BLK, DH), bf16),
+            pltpu.VMEM((2, PEERS, TILE_ROWS, 2 * DH), f32),
+            pltpu.VMEM((2, PEERS, TILE_ROWS, DH), f32),
+            pltpu.VMEM((PEERS, 1, 128), f32),
+            dma((8,)),
+            dma((SLOTS, 4, 2)),
+            dma((SLOTS, 4, 2)),
+            dma((PEERS,)),
+            dma((PEERS,)),
+            dma((2, PEERS)),
+            dma((2, PEERS)),
+            dma((PEERS,)),
+            dma((PEERS,)),
+        ],
+        compiler_params=pltpu.CompilerParams(
+            collective_id=1, has_side_effects=True, vmem_limit_bytes=56 * 2**20
+        ),
+        name="exchange_attend",
+    )(send, place, limit, factor, flag, queries, span_keys, span_values, cache_keys, cache_values)
+
+
+def per_device(*arrays):
+    attended, over = routed(*arrays)
+    return lax.cond(over[0, 0] > 0, lambda: exchange_all(*arrays), lambda: attended)
+
+
 def solution(mesh):
     placed = (
         P(None, "seq", "inter", None),

time: 356 us -> 104 us (0.29)
  waiting for transfers between devices: 146 us -> 0 us
  Pallas kernels: 0 us -> 84.6 us
  local copies, waits for them, and re-layouts: 83.7 us -> 2.4 us
  blocking collectives: 44.5 us -> 0 us
  other arithmetic: 31.8 us -> 2.08 us
  matrix products: 24.4 us -> 0 us
  starting transfers between devices: 10.2 us -> 0 us
    all_to_all x2 -> x0, waiting for transfers between devices: 108 us -> none  [the longest x1 108 us: per_device(): lax.all_to_all(packed, 'seq', split_axis=0, concat_axis=0, tiled=True)]
    pallas_call x0 -> x3, Pallas kernels: none -> 84.6 us  [the longest x1 64.9 us: routed(): pl.pallas_call(main_kernel, out_shape=(jax.ShapeDtypeStruct(queries.shape...]
    all_gather x3 -> x0, blocking collectives: 44.5 us -> none  [the longest x1 18.5 us: per_device(): listed = lax.all_gather(selections, 'seq', axis=1, tiled=True)]
    all_gather x3 -> x0, waiting for transfers between devices: 38.1 us -> none  [the longest x1 38.1 us: per_device(): lax.all_gather(fetched_kv, 'inter', axis=0, tiled=True)]
    broadcast_in_dim x10 -> x0, local copies, waits for them, and re-layouts: 34.5 us -> none  [the longest x4 33.8 us: attend(): jnp.where(allowed, jnp.exp(jnp.where(allowed, scores, top_score) - top_sc...]
    dot_general x10 -> x0, matrix products: 24.4 us -> none  [the longest x6 11.7 us: attend(): jnp.dot(piece, chosen_values[index], preferred_element_type=jnp.float32)]
    reduce_sum x4 -> x0, other arithmetic: 18.8 us -> none  [the longest x2 18.5 us: attend(): total = jnp.sum(weights, axis=-1, keepdims=True)]
    gather x7 -> x0, local copies, waits for them, and re-layouts: 17.8 us -> none  [the longest x1 5.24 us: per_device(): picked_values = stored_values[slot_block, :, group_ids, :]]
  transfers between devices with their start and end apart: 5 -> 0, of which waited for: 2 -> 0; matrix products, arithmetic and copies ran while one was open for 4% -> 0% of each run, Pallas kernels for 0% -> 0%
where the time goes in v1:
time: 104 us
  Pallas kernels  84.6 us (81%)
  between operations  14.8 us (14%)
  local copies, waits for them, and re-layouts  2.4 us (2%)
  other arithmetic  2.08 us (2%)
    pallas_call x1, Pallas kernels, routed(): pl.pallas_call(main_kernel, out_shape=(jax.ShapeDtypeStruct(queries.shape...  64.9 us
    pallas_call x1, Pallas kernels, routed(): pl.pallas_call(lists_kernel, out_shape=(jax.ShapeDtypeStruct((NODES, 1, 1...  11.4 us
    pallas_call x1, Pallas kernels, routed(): pl.pallas_call(plan_kernel, out_shape=(jax.ShapeDtypeStruct((4 * SLOTS,),...  8.26 us
    unnamed x13, local copies, waits for them, and re-layouts  2.31 us

profile of v1, /device:TPU:1, one launch (start us, length us, event | category | flops | bytes accessed | tf_op | source)
XLA Modules:
  0.0 104.1 jit_solution(10417051757280227736)
XLA Ops:
  6.5 0.0 copy-start.1
  6.5 0.0 copy-start
  6.5 0.0 copy-start.9
  6.5 0.0 copy-start.4
  6.5 0.0 copy-start.5
  6.6 0.0 copy-start.6
  6.6 0.8 bitcast_convert_fusion.3
  7.4 0.7 convert_reduce_fusion
  8.1 0.1 convert_element_type.101
  8.1 0.6 fusion.51.x_ref
  8.7 11.4 %lists.1 = (f32[16,1,128]{2,1,0:T(1,128)}, s32[16,1,128]{2,1,0:T(1,128)}) custom-call(f32[1,128]{1,0:T(1,128)} %fusion.51.x_ref), custom_call_target="tpu_custom_call" | custom-call | tf_op jit(solution)/shard_map/lists/pallas_call | solution.py:560
  20.8 8.3 %plan.1 = (s32[28]{0:T(128)}, s32[8]{0:T(128)}, s32[8]{0:T(128)}, f32[16]{0:T(128)}, f32[1,128]{1,0:T(1,128)}) custom-call(s32[16,1,128]{2,1,0:T(1,128)} %get-tuple-element.97.lists, f32[16,1,128]{2,1,0:T(1,128)} %get-tuple-element.98.scales, s32[1]{0:T(128)S(6)} %copy.172.start, s32[8704]{0:T(1024)} %constant.106.clone.tab), custom_call_target="tpu_custom_call" | custom-call | tf_op jit(solution)/shard_map/plan/pallas_call | solution.py:572
  29.0 64.9 %exchange_attend.1 = (bf16[2,1,64,4096]{3,2,1,0:T(8,128)(2,1)}, f32[1,128]{1,0:T(1,128)}) custom-call(s32[28]{0:T(128)} %get-tuple-element.99.send, s32[8]{0:T(128)} %get-tuple-element.100.place, s32[8]{0:T(128)} %get-tuple-element.101.limit, f32[16]{0:T(128)} %get-tuple-element.102.factor, f32[1,128]{1,0:T(1,128)} %get-tuple-element.103.flag, ...), custom_call_target="tpu_custom_call" | custom-call | tf_op jit(solution)/shard_map/exchange_attend/pallas_call | solution.py:592
  94.7 0.0 copy-done.1
  94.7 0.0 copy-done
  94.7 0.0 copy-done.9
  94.7 0.0 copy-done.4
  94.7 0.0 copy-done.5
  94.7 0.0 copy-done.6
  94.7 0.2 conditional.1
  95.0 2.3 %copy.174 = bf16[2,1,64,4096]{3,2,1,0:T(8,128)(2,1)} copy(bf16[2,1,64,4096]{3,2,1,0:T(8,128)(2,1)} %get-tuple-element.106) | data formatting | bytes 2097152
Async XLA Ops:
  6.5 88.2 %copy-start.1 = (bf16[32,1,1]{0,2,1:T(2,128)(2,1)S(1)}, bf16[32,1,1]{0,2,1:T(2,128)(2,1)}, u32[]{:S(2)}) copy-start(bf16[32,1,1]{0,2,1:T(2,128)(2,1)} %param.19) | copy-start | bytes 196
  6.5 88.2 %copy-start = (bf16[32,1,1]{0,2,1:T(2,128)(2,1)S(1)}, bf16[32,1,1]{0,2,1:T(2,128)(2,1)}, u32[]{:S(2)}) copy-start(bf16[32,1,1]{0,2,1:T(2,128)(2,1)} %param.20) | copy-start | bytes 196
  6.5 88.2 %copy-start.9 = (s32[2,1,1,3]{3,2,1,0:T(1,128)S(1)}, s32[2,1,1,3]{3,2,1,0:T(1,128)}, u32[]{:S(2)}) copy-start(s32[2,1,1,3]{3,2,1,0:T(1,128)} %param.21) | copy-start | bytes 76
  6.5 88.2 %copy-start.4 = (bf16[2,1,64,4096]{3,2,1,0:T(8,128)(2,1)S(1)}, bf16[2,1,64,4096]{3,2,1,0:T(8,128)(2,1)}, u32[]{:S(2)}) copy-start(bf16[2,1,64,4096]{3,2,1,0:T(8,128)(2,1)} %q.1) | copy-start | bytes 3145732
  6.5 88.2 %copy-start.5 = (bf16[2,1,512,128]{3,2,1,0:T(8,128)(2,1)S(1)}, bf16[2,1,512,128]{3,2,1,0:T(8,128)(2,1)}, u32[]{:S(2)}) copy-start(bf16[2,1,512,128]{3,2,1,0:T(8,128)(2,1)} %sk_hbm.1) | copy-start | bytes 786436
  6.6 88.2 %copy-start.6 = (bf16[2,1,512,128]{3,2,1,0:T(8,128)(2,1)S(1)}, bf16[2,1,512,128]{3,2,1,0:T(8,128)(2,1)}, u32[]{:S(2)}) copy-start(bf16[2,1,512,128]{3,2,1,0:T(8,128)(2,1)} %sv_hbm.1) | copy-start | bytes 786436

commit v2 on v1

--- a/solution.py
+++ b/solution.py
@@ -15,9 +15,11 @@
 SIDE = 4
 NODES = SIDE * SIDE
 ROWS_KV = 32
-SLOTS = 7
-SLOTS_FIRST = 6
+SLOTS = 6
+SLOTS_FIRST = 5
 CANDS = 8
+TRIES = 10
+LOAD = 256
 PEERS = 8
 QROWS = BLK // PEERS
 WIDE = HG * DH
@@ -73,103 +75,51 @@
     return (summed.reshape(row_count, head_count, head_dim) / total).astype(jnp.bfloat16)
 
 
-def exchange_all(
-    queries,
-    span_keys,
-    span_values,
-    cache_keys,
-    cache_values,
-    block_key_scales,
-    value_scales,
-    selections,
-    start,
-):
+def padded(queries, span_keys, span_values, cache_keys, cache_values, start, lists, scales):
     blocks_here = queries.shape[0]
-    groups_here = selections.shape[2]
-    stored_blocks = cache_keys.shape[0]
-    seq_count = lax.axis_size("seq")
     seq_rank = lax.axis_index("seq")
-    item_count = 3 * blocks_here
-    capacity = max(2, (item_count + seq_count - 1) // seq_count)
-    cutoff = start[0]
-    listed = lax.all_gather(selections, "seq", axis=1, tiled=True)
-    wanted = jnp.transpose(listed, (1, 2, 0, 3)).reshape(seq_count, groups_here, item_count)
-    owner_rank = wanted % seq_count
-    local_row = wanted // seq_count
+    wanted = lists[:, 0, 64:70]
+    owner_rank = wanted % NODES
+    local_row = wanted // NODES
     is_mine = (owner_rank == seq_rank).astype(jnp.int32)
-    ranking = jnp.cumsum(is_mine, axis=2) - 1
-    slot_ids = jnp.arange(capacity, dtype=jnp.int32)
+    ranking = jnp.cumsum(is_mine, axis=1) - 1
+    slot_ids = jnp.arange(2, dtype=jnp.int32)
     slot_hits = (is_mine[..., None] == 1) & (ranking[..., None] == slot_ids)
-    slot_block = jnp.sum(jnp.where(slot_hits, local_row[..., None], 0), axis=2)
-    group_ids = jnp.arange(groups_here, dtype=jnp.int32)[None, :, None]
-    stored_keys = cache_keys[:, 0].reshape(stored_blocks, BLK, groups_here, DH)
-    stored_values = cache_values[:, 0].reshape(stored_blocks, BLK, groups_here, DH)
-    picked_keys = stored_keys[slot_block, :, group_ids, :]
-    picked_values = stored_values[slot_block, :, group_ids, :]
-    packed = jnp.concatenate([picked_keys, picked_values], axis=-1)
-    scale_pack = jnp.stack(
-        [block_key_scales[:, 0][slot_block, group_ids], value_scales[:, 0][slot_block, group_ids]],
-        axis=-1,
-    )
-    got_blocks, got_scales = (
-        lax.all_to_all(packed, "seq", split_axis=0, concat_axis=0, tiled=True),
-        lax.all_to_all(scale_pack, "seq", split_axis=0, concat_axis=0, tiled=True),
-    )
-    own_lists = jnp.transpose(selections[:, 0], (1, 0, 2)).reshape(groups_here, item_count)
-    own_owner = own_lists % seq_count
-    item_ids = jnp.arange(item_count, dtype=jnp.int32)
-    earlier = (own_owner[:, :, None] == own_owner[:, None, :]) & (
-        item_ids[None, None, :] < item_ids[None, :, None]
-    )
-    slot_of = jnp.sum(earlier.astype(jnp.int32), axis=2)
-    group_rows = jnp.arange(groups_here, dtype=jnp.int32)[:, None]
-    fetched_kv = got_blocks[own_owner, group_rows, slot_of]
-    fetched_sc = got_scales[own_owner, group_rows, slot_of]
-    inter_rank = lax.axis_index("inter")
-    all_kv, all_sc = (
-        lax.all_gather(fetched_kv, "inter", axis=0, tiled=True),
-        lax.all_gather(fetched_sc, "inter", axis=0, tiled=True),
-    )
-    all_lists = lax.all_gather(selections, "inter", axis=2, tiled=True)
-    whole_keys, whole_values = (
-        lax.all_gather(span_keys, "inter", axis=3, tiled=True),
-        lax.all_gather(span_values, "inter", axis=3, tiled=True),
-    )
-    group_total = all_kv.shape[0]
-    row_count = queries.shape[2]
-    positions = inter_rank * row_count + jnp.arange(row_count, dtype=jnp.int32)
-    query_all = queries[:, 0].reshape(blocks_here, row_count, group_total, HG, DH)
-    keys_all = whole_keys[:, 0].reshape(blocks_here, BLK, group_total, DH)
-    values_all = whole_values[:, 0].reshape(blocks_here, BLK, group_total, DH)
-    pack_all = jnp.transpose(
-        all_kv.reshape(group_total, blocks_here, 3, BLK, 2 * DH), (1, 0, 2, 3, 4)
-    )
-    scale_all = jnp.transpose(all_sc.reshape(group_total, blocks_here, 3, 2), (1, 0, 2, 3))
-    ids_all = all_lists[:, 0]
+    slot_block = jnp.sum(jnp.where(slot_hits, local_row[..., None], 0), axis=1)
+    packed = jnp.concatenate([cache_keys[slot_block, 0], cache_values[slot_block, 0]], axis=-1)
+    got_blocks = lax.all_to_all(packed, "seq", split_axis=0, concat_axis=0, tiled=True)
+    own_list = wanted[seq_rank]
+    own_owner = own_list % NODES
+    item_ids = jnp.arange(6, dtype=jnp.int32)
+    earlier = (own_owner[:, None] == own_owner[None, :]) & (item_ids[None, :] < item_ids[:, None])
+    slot_of = jnp.sum(earlier.astype(jnp.int32), axis=1)
+    fetched = got_blocks[own_owner, slot_of].reshape(blocks_here, 3, BLK, 2 * DH)
+    row = own_list // NODES
+    key_scale = scales[own_owner, 0, row].reshape(blocks_here, 3)
+    value_scale = scales[own_owner, 0, ROWS_KV + row].reshape(blocks_here, 3)
+    whole = lax.all_to_all(queries, "inter", split_axis=3, concat_axis=2, tiled=True)
+    positions = jnp.arange(BLK, dtype=jnp.int32)
 
     def attend_block(inputs):
-        query_vector, keys_one, values_one, pack_one, scale_one, ids_one = inputs
-
-        def group_results(query_g, keys_g, values_g, pack_g, scale_g, ids_g):
-            return attend(
-                query_g,
-                keys_g,
-                values_g,
-                pack_g[..., :DH],
-                pack_g[..., DH:],
-                scale_g[:, 0],
-                scale_g[:, 1],
-                ids_g,
-                cutoff,
-                positions,
-            )
-
-        return jax.vmap(group_results, in_axes=(1, 1, 1, 0, 0, 0), out_axes=1)(
-            query_vector, keys_one, values_one, pack_one, scale_one, ids_one
-        )
-
-    result = lax.map(attend_block, (query_all, keys_all, values_all, pack_all, scale_all, ids_all))
-    return result.reshape(blocks_here, 1, row_count, group_total * HG * DH)
+        query, keys, values, pack, key_scale, value_scale, ids = inputs
+        return attend(
+            query, keys, values, pack[..., :DH], pack[..., DH:], key_scale, value_scale, ids, start[0], positions
+        )
+
+    result = lax.map(
+        attend_block,
+        (
+            whole.reshape(blocks_here, BLK, HG, DH),
+            span_keys[:, 0],
+            span_values[:, 0],
+            fetched,
+            key_scale,
+            value_scale,
+            own_list.reshape(blocks_here, 3),
+        ),
+    )
+    result = result.reshape(blocks_here, 1, BLK, WIDE)
+    return lax.all_to_all(result, "inter", split_axis=2, concat_axis=3, tiled=True)
 
 
 def path_tables():
@@ -194,29 +144,34 @@
             found = paths(owner, dest)
             pair = owner * NODES + dest
             dist[pair] = len(found[0])
-            count = min(CANDS, len(found))
+            count = min(6, len(found))
             for c in range(count):
                 path = found[c * len(found) // count]
                 table[pair, c, : len(path)] = path
     slot_of = np.zeros((256,), np.int32)
     for bit in range(8):
-        slot_of[1 << bit] = bit
+        slot_of[(2 << bit) - 1] = bit
     return np.concatenate([table.reshape(-1), dist, slot_of])
 
 
 TABLES = path_tables()
 DIST_AT = NODES * NODES * CANDS * 4
 SLOT_AT = DIST_AT + NODES * NODES
-CHOICES = {4: CANDS, 3: 6, 2: 2, 1: 1}
-
-
-def lists_kernel(x_ref, f_ref, i_ref, buf, send_sem, recv_sem):
+CHOICES = {4: 6, 3: 6, 2: 2, 1: 1}
+
+
+def lists_kernel(ks_ref, vs_ref, sel_ref, f_ref, i_ref, x_ref, buf, send_sem, recv_sem):
     s, r = lax.axis_index("seq"), lax.axis_index("inter")
     barrier = pltpu.get_barrier_semaphore()
     for k in range(1, NODES):
         pl.semaphore_signal(
             barrier, inc=1, device_id=(lax.rem(s + k, NODES), r), device_id_type=MESH
         )
+    x_ref[...] = jnp.zeros_like(x_ref)
+    x_ref[0:1, 0:ROWS_KV] = ks_ref[...].astype(jnp.float32)
+    x_ref[0:1, ROWS_KV : 2 * ROWS_KV] = vs_ref[...].astype(jnp.float32)
+    for j in range(2):
+        x_ref[0:1, 64 + 3 * j : 67 + 3 * j] = sel_ref[j : j + 1].astype(jnp.float32)
     pl.semaphore_wait(barrier, NODES - 1)
     copies = []
     for k in range(1, NODES):
@@ -239,17 +194,18 @@
 
 
 def plan_kernel(
-    lists, scales, start, tab, send, place, limit, factor, flag, occ, bucket, cnt, tbl, posn
+    lists, scales, start, tab, send, place, limit, factor, flag, occ, bucket, cnt, tbl, posn, front
 ):
     me = lax.axis_index("seq")
 
-    def clear(i, _):
-        occ[i] = 0
-        return 0
-
-    lax.fori_loop(0, NODES * 4, clear, 0, unroll=8)
-    for i in range(9):
-        cnt[i] = 0
+    def clear(ref, count):
+        def step(i, _):
+            ref[i] = 0
+            return 0
+
+        lax.fori_loop(0, count, step, 0, unroll=8)
+
+    clear(front, NODES * 8)
     for t in range(SLOTS):
         for d in range(4):
             tbl[(me * 4 + d) * 8 + t] = 0
@@ -259,66 +215,81 @@
             block = lists[dest, 0, 64 + jk]
             owner = block & (NODES - 1)
             steps = tab[DIST_AT + owner * NODES + dest]
-            posn[dest * 8 + jk] = block >> 4
-            kind = jnp.where(steps == 0, 8, (jk // 3) * 4 + 4 - steps)
+            item = dest * 8 + jk
+            posn[item] = block >> 4
+            phase = jnp.where(front[item] > 0, 0, 1 + jk // 3)
+            kind = jnp.where(steps == 0, 12, phase * 4 + 4 - steps)
             at = cnt[kind]
-            bucket[kind * 48 + at] = dest * 8 + jk
+            bucket[kind * 96 + at] = item
             cnt[kind] = at + 1
         return 0
 
-    lax.fori_loop(0, NODES, sort_dest, 0)
-
     def chain(base, hops):
-        links, marks = [], []
-        seen = None
+        links, ends = [], []
+        seen, words = 0, 0
         for h in range(hops):
             link = tab[base + h]
-            used = occ[link]
-            if seen is not None:
-                used = used | seen
-            mark = (~used) & (used + 1)
-            seen = mark | (mark - 1)
+            word = occ[link]
+            used = word | seen
+            seen = used ^ (used + 1)
+            words = words + word
             links.append(link)
-            marks.append(mark)
-        return links, marks
-
-    over = jnp.int32(0)
-    for j in range(2):
-        bound = 1 << (SLOTS_FIRST if j == 0 else SLOTS)
-        for hops in (4, 3, 2, 1):
-            kind = j * 4 + 4 - hops
-
-            def route(i, over, kind=kind, hops=hops, bound=bound):
-                item = bucket[kind * 48 + i]
-                dest = item >> 3
-                block = lists[dest, 0, 64 + (item & 7)]
-                owner = block & (NODES - 1)
-                base = (owner * NODES + dest) * (CANDS * 4)
-                best_at, best = base, None
-                for c in range(CHOICES[hops]):
-                    cost = chain(base + 4 * c, hops)[1][-1]
-                    if best is None:
-                        best = cost
-                    else:
-                        best_at = jnp.where(cost < best, base + 4 * c, best_at)
-                        best = jnp.minimum(cost, best)
-                fits = best < bound
-
-                @pl.when(fits)
-                def _():
-                    links, marks = chain(best_at, hops)
-                    source = block >> 4
-                    for link, mark in zip(links, marks):
-                        occ[link] = occ[link] | mark
-                        slot = tab[SLOT_AT + mark]
-                        tbl[link * 8 + slot] = source
-                        source = ROWS_KV + 4 * slot + (link & 3)
-                    posn[item] = source
-
-                return over | jnp.where(fits, 0, 1)
-
-            over = lax.fori_loop(0, cnt[kind], route, over)
-
+            ends.append(seen)
+        return links, ends, words
+
+    def attempt(carry):
+        clear(occ, NODES * 4)
+        for kind in range(13):
+            cnt[kind] = 0
+        lax.fori_loop(0, NODES, sort_dest, 0)
+
+        def run_phase(phase, missed):
+            for hops in (4, 3, 2, 1):
+                kind = phase * 4 + 4 - hops
+
+                def route(i, missed, kind=kind, hops=hops):
+                    item = bucket[kind * 96 + i]
+                    dest = item >> 3
+                    jk = item & 7
+                    block = lists[dest, 0, 64 + jk]
+                    owner = block & (NODES - 1)
+                    base = (owner * NODES + dest) * (CANDS * 4)
+                    best_at, best = base, None
+                    for c in range(CHOICES[hops]):
+                        _, ends, words = chain(base + 4 * c, hops)
+                        cost = (ends[-1] << 16) + words
+                        if best is None:
+                            best = cost
+                        else:
+                            best_at = jnp.where(cost < best, base + 4 * c, best_at)
+                            best = jnp.minimum(cost, best)
+                    fits = best < jnp.where(jk < 3, 1 << (16 + SLOTS_FIRST), 1 << (16 + SLOTS))
+
+                    @pl.when(fits)
+                    def _():
+                        links, ends, _ = chain(best_at, hops)
+                        source = block >> 4
+                        for link, end in zip(links, ends):
+                            occ[link] = (occ[link] | ((end + 1) >> 1)) + LOAD
+                            slot = tab[SLOT_AT + end]
+                            tbl[link * 8 + slot] = source
+                            source = ROWS_KV + 4 * slot + (link & 3)
+                        posn[item] = source
+
+                    @pl.when(jnp.logical_not(fits))
+                    def _():
+                        front[item] = 1
+
+                    return missed + jnp.where(fits, 0, 1)
+
+                missed = lax.fori_loop(0, cnt[kind], route, missed)
+            return missed
+
+        return lax.fori_loop(0, 3, run_phase, jnp.int32(0)), carry[1] + 1
+
+    missed, _ = lax.while_loop(
+        lambda carry: (carry[0] > 0) & (carry[1] < TRIES), attempt, (jnp.int32(1), jnp.int32(0))
+    )
     for t in range(SLOTS):
         for d in range(4):
             send[t * 4 + d] = tbl[(me * 4 + d) * 8 + t]
@@ -330,7 +301,7 @@
         limit[jk] = start[0] - block * BLK
         factor[jk] = scales[owner, 0, row] * (LOG2E / math.sqrt(DH))
         factor[8 + jk] = scales[owner, 0, ROWS_KV + row]
-    flag[...] = jnp.full((1, 128), over, jnp.int32).astype(jnp.float32)
+    flag[...] = jnp.full((1, 128), missed, jnp.int32).astype(jnp.float32)
 
 
 def main_kernel(
@@ -545,7 +516,7 @@
             o_copy(j, k).wait()
 
 
-def routed(
+def per_device(
     queries, span_keys, span_values, cache_keys, cache_values, key_scales, value_scales, selections, start
 ):
     f32, i32, bf16 = jnp.float32, jnp.int32, jnp.bfloat16
@@ -553,22 +524,23 @@
     vmem = pl.BlockSpec(memory_space=pltpu.VMEM)
     hbm = pl.BlockSpec(memory_space=pl.ANY)
     dma = pltpu.SemaphoreType.DMA
-    row = jnp.concatenate(
-        [key_scales.reshape(-1).astype(f32), value_scales.reshape(-1).astype(f32), selections.reshape(-1).astype(f32)]
-    )
-    row = jnp.pad(row, (0, 128 - row.shape[0])).reshape(1, 128)
     scales, lists = pl.pallas_call(
         lists_kernel,
         out_shape=(
             jax.ShapeDtypeStruct((NODES, 1, 128), f32),
             jax.ShapeDtypeStruct((NODES, 1, 128), i32),
         ),
-        in_specs=[vmem],
+        in_specs=[vmem] * 3,
         out_specs=(vmem, vmem),
-        scratch_shapes=[pltpu.VMEM((NODES, 1, 128), f32), dma((NODES,)), dma((NODES,))],
+        scratch_shapes=[
+            pltpu.VMEM((1, 128), f32),
+            pltpu.VMEM((NODES, 1, 128), f32),
+            dma((NODES,)),
+            dma((NODES,)),
+        ],
         compiler_params=pltpu.CompilerParams(collective_id=0, has_side_effects=True),
         name="lists",
-    )(row)
+    )(key_scales.reshape(1, ROWS_KV), value_scales.reshape(1, ROWS_KV), selections.reshape(2, 3))
     send, place, limit, factor, flag = pl.pallas_call(
         plan_kernel,
         out_shape=(
@@ -582,14 +554,15 @@
         out_specs=(smem, smem, smem, smem, vmem),
         scratch_shapes=[
             pltpu.SMEM((NODES * 4,), i32),
-            pltpu.SMEM((9 * 48 + 96,), i32),
+            pltpu.SMEM((13 * 96,), i32),
             pltpu.SMEM((16,), i32),
             pltpu.SMEM((NODES * 4 * 8,), i32),
+            pltpu.SMEM((NODES * 8,), i32),
             pltpu.SMEM((NODES * 8,), i32),
         ],
         name="plan",
     )(lists, scales, start, jnp.asarray(TABLES))
-    return pl.pallas_call(
+    attended, over = pl.pallas_call(
         main_kernel,
         out_shape=(
             jax.ShapeDtypeStruct(queries.shape, bf16),
@@ -624,11 +597,11 @@
         ),
         name="exchange_attend",
     )(send, place, limit, factor, flag, queries, span_keys, span_values, cache_keys, cache_values)
-
-
-def per_device(*arrays):
-    attended, over = routed(*arrays)
-    return lax.cond(over[0, 0] > 0, lambda: exchange_all(*arrays), lambda: attended)
+    return lax.cond(
+        over[0, 0] > 0,
+        lambda: padded(queries, span_keys, span_values, cache_keys, cache_values, start, lists, scales),
+        lambda: attended,
+    )
 
 
 def solution(mesh):

time: 104 us -> 89.6 us (0.86)
  between operations: 14.8 us -> 1.31 us
  other arithmetic: 2.08 us -> 0 us
    convert_element_type x2 -> x0, other arithmetic: 1.49 us -> none  [the longest x1 0.8 us: routed(): value_scales.reshape(-1).astype(f32)]
    unnamed x13 -> x3, local copies, waits for them, and re-layouts: 2.31 us -> 2.29 us
where the time goes in v2:
time: 89.6 us; the launch traced here: 89 us
  Pallas kernels  85.2 us (95%)
  local copies, waits for them, and re-layouts  2.29 us (3%)
  between operations  1.31 us (1%)
    pallas_call x1, Pallas kernels, per_device(): pl.pallas_call(main_kernel, out_shape=(jax.ShapeDtypeStruct(queries.shape...  65.5 us
    pallas_call x1, Pallas kernels, per_device(): pl.pallas_call(lists_kernel, out_shape=(jax.ShapeDtypeStruct((NODES, 1, 1...  10.8 us
    pallas_call x1, Pallas kernels, per_device(): pl.pallas_call(plan_kernel, out_shape=(jax.ShapeDtypeStruct((4 * SLOTS,),...  8.79 us
    unnamed x3, local copies, waits for them, and re-layouts  2.29 us

profile of v2, /device:TPU:1, one launch (start us, length us, event | category | flops | bytes accessed | tf_op | source)
XLA Modules:
  0.0 89.0 jit_solution(12085555276755773748)
XLA Ops:
  0.0 10.8 %lists.1 = (f32[16,1,128]{2,1,0:T(1,128)S(1)}, s32[16,1,128]{2,1,0:T(1,128)S(1)}) custom-call(bf16[1,32]{1,0:T(2,128)(2,1)} %bitcast.168, bf16[1,32]{1,0:T(2,128)(2,1)} %bitcast.169, s32[2,3]{1,0:T(2,128)} %bitcast.167), custom_call_target="tpu_custom_call" | custom-call | tf_op jit(solution)/shard_map/lists/pallas_call | solution.py:527
  11.5 8.8 %plan.1 = (s32[24]{0:T(128)}, s32[8]{0:T(128)}, s32[8]{0:T(128)}, f32[16]{0:T(128)}, f32[1,128]{1,0:T(1,128)}) custom-call(s32[16,1,128]{2,1,0:T(1,128)S(1)} %get-tuple-element.99.lists, f32[16,1,128]{2,1,0:T(1,128)S(1)} %get-tuple-element.100.scales, s32[1]{0:T(128)S(6)} %copy.150.start, s32[8704]{0:T(1024)} %constant.114.clone.tab), custom_call_target="tpu_custom_call" | custom-call | tf_op jit(solution)/shard_map/plan/pallas_call | solution.py:544
  20.3 0.0 copy-start.1
  20.3 65.5 %exchange_attend.1 = (bf16[2,1,64,4096]{3,2,1,0:T(8,128)(2,1)}, f32[1,128]{1,0:T(1,128)}) custom-call(s32[24]{0:T(128)} %get-tuple-element.101.send, s32[8]{0:T(128)} %get-tuple-element.102.place, s32[8]{0:T(128)} %get-tuple-element.103.limit, f32[16]{0:T(128)} %get-tuple-element.104.factor, f32[1,128]{1,0:T(1,128)} %get-tuple-element.105.flag, ...), custom_call_target="tpu_custom_call" | custom-call | tf_op jit(solution)/shard_map/exchange_attend/pallas_call | solution.py:565
  86.5 0.0 copy-done.1
  86.5 0.2 conditional.1
  86.7 2.3 %copy.152 = bf16[2,1,64,4096]{3,2,1,0:T(8,128)(2,1)} copy(bf16[2,1,64,4096]{3,2,1,0:T(8,128)(2,1)} %bitcast.166) | data formatting | bytes 2097152
Async XLA Ops:
  20.3 66.2 %copy-start.1 = (bf16[2,1,64,4096]{3,2,1,0:T(8,128)(2,1)S(1)}, bf16[2,1,64,4096]{3,2,1,0:T(8,128)(2,1)}, u32[]{:S(2)}) copy-start(bf16[2,1,64,4096]{3,2,1,0:T(8,128)(2,1)} %q.1) | copy-start | bytes 3145732

commit v3 on v2

--- a/solution.py
+++ b/solution.py
@@ -16,14 +16,16 @@
 NODES = SIDE * SIDE
 ROWS_KV = 32
 SLOTS = 6
-SLOTS_FIRST = 5
-CANDS = 8
+SLOTS_FIRST = 4
+CANDS = 6
 TRIES = 10
 LOAD = 256
 PEERS = 8
 QROWS = BLK // PEERS
 WIDE = HG * DH
-TILE_ROWS = HG * QROWS
+CHIPS = PEERS // 2
+CROWS = 2 * QROWS
+TILE_ROWS = HG * CROWS
 POOL = ROWS_KV + 4 * SLOTS
 LOG2E = 1.4426950408889634
 NEG = -1e30
@@ -75,10 +77,10 @@
     return (summed.reshape(row_count, head_count, head_dim) / total).astype(jnp.bfloat16)
 
 
-def padded(queries, span_keys, span_values, cache_keys, cache_values, start, lists, scales):
+def padded(queries, span_keys, span_values, cache_keys, cache_values, start, rows):
     blocks_here = queries.shape[0]
     seq_rank = lax.axis_index("seq")
-    wanted = lists[:, 0, 64:70]
+    wanted = rows[:, 0, 64:70].astype(jnp.int32)
     owner_rank = wanted % NODES
     local_row = wanted // NODES
     is_mine = (owner_rank == seq_rank).astype(jnp.int32)
@@ -95,8 +97,8 @@
     slot_of = jnp.sum(earlier.astype(jnp.int32), axis=1)
     fetched = got_blocks[own_owner, slot_of].reshape(blocks_here, 3, BLK, 2 * DH)
     row = own_list // NODES
-    key_scale = scales[own_owner, 0, row].reshape(blocks_here, 3)
-    value_scale = scales[own_owner, 0, ROWS_KV + row].reshape(blocks_here, 3)
+    key_scale = rows[own_owner, 0, row].reshape(blocks_here, 3)
+    value_scale = rows[own_owner, 0, ROWS_KV + row].reshape(blocks_here, 3)
     whole = lax.all_to_all(queries, "inter", split_axis=3, concat_axis=2, tiled=True)
     positions = jnp.arange(BLK, dtype=jnp.int32)
 
@@ -137,17 +139,17 @@
         ways = [w for w, ok in enumerate((rx in (1, 2), rx in (2, 3), rz in (1, 2), rz in (2, 3))) if ok]
         return [[here * 4 + w] + rest for w in ways for rest in paths(move(here, w), there)]
 
-    table = np.zeros((NODES * NODES, CANDS, 4), np.int32)
+    table = np.zeros((NODES * NODES, CANDS), np.int32)
     dist = np.zeros((NODES * NODES,), np.int32)
     for owner in range(NODES):
         for dest in range(NODES):
             found = paths(owner, dest)
             pair = owner * NODES + dest
             dist[pair] = len(found[0])
-            count = min(6, len(found))
+            count = min(CANDS, len(found))
             for c in range(count):
                 path = found[c * len(found) // count]
-                table[pair, c, : len(path)] = path
+                table[pair, c] = sum(link << (8 * hop) for hop, link in enumerate(path))
     slot_of = np.zeros((256,), np.int32)
     for bit in range(8):
         slot_of[(2 << bit) - 1] = bit
@@ -155,12 +157,12 @@
 
 
 TABLES = path_tables()
-DIST_AT = NODES * NODES * CANDS * 4
+DIST_AT = NODES * NODES * CANDS
 SLOT_AT = DIST_AT + NODES * NODES
-CHOICES = {4: 6, 3: 6, 2: 2, 1: 1}
-
-
-def lists_kernel(ks_ref, vs_ref, sel_ref, f_ref, i_ref, x_ref, buf, send_sem, recv_sem):
+CHOICES = {4: CANDS, 3: CANDS, 2: 2, 1: 1}
+
+
+def lists_kernel(ks_ref, vs_ref, sel_ref, out_ref, x_ref, buf, send_sem, recv_sem):
     s, r = lax.axis_index("seq"), lax.axis_index("inter")
     barrier = pltpu.get_barrier_semaphore()
     for k in range(1, NODES):
@@ -188,13 +190,11 @@
     buf[s] = x_ref[...]
     for copy in copies:
         copy.wait()
-    got = buf[...]
-    f_ref[...] = got
-    i_ref[...] = got.astype(jnp.int32)
+    out_ref[...] = buf[...]
 
 
 def plan_kernel(
-    lists, scales, start, tab, send, place, limit, factor, flag, occ, bucket, cnt, tbl, posn, front
+    rows, start, tab, send, place, limit, factor, flag, occ, bucket, cnt, tbl, posn, front
 ):
     me = lax.axis_index("seq")
 
@@ -212,30 +212,20 @@
 
     def sort_dest(dest, _):
         for jk in range(6):
-            block = lists[dest, 0, 64 + jk]
-            owner = block & (NODES - 1)
-            steps = tab[DIST_AT + owner * NODES + dest]
+            block = rows[dest, 0, 64 + jk].astype(jnp.int32)
+            row = block >> 4
+            pair = (block & (NODES - 1)) * NODES + dest
+            steps = jnp.where(block * BLK < start[0], tab[DIST_AT + pair], 0)
+            only = jnp.where(steps == 1, tab[pair * CANDS], NODES * 4)
+            occ[only] = occ[only] + LOAD
             item = dest * 8 + jk
-            posn[item] = block >> 4
+            posn[item] = row
             phase = jnp.where(front[item] > 0, 0, 1 + jk // 3)
             kind = jnp.where(steps == 0, 12, phase * 4 + 4 - steps)
             at = cnt[kind]
-            bucket[kind * 96 + at] = item
+            bucket[kind * 96 + at] = (pair * CANDS) | (row << 16) | (item << 24)
             cnt[kind] = at + 1
         return 0
-
-    def chain(base, hops):
-        links, ends = [], []
-        seen, words = 0, 0
-        for h in range(hops):
-            link = tab[base + h]
-            word = occ[link]
-            used = word | seen
-            seen = used ^ (used + 1)
-            words = words + word
-            links.append(link)
-            ends.append(seen)
-        return links, ends, words
 
     def attempt(carry):
         clear(occ, NODES * 4)
@@ -248,39 +238,42 @@
                 kind = phase * 4 + 4 - hops
 
                 def route(i, missed, kind=kind, hops=hops):
-                    item = bucket[kind * 96 + i]
-                    dest = item >> 3
-                    jk = item & 7
-                    block = lists[dest, 0, 64 + jk]
-                    owner = block & (NODES - 1)
-                    base = (owner * NODES + dest) * (CANDS * 4)
-                    best_at, best = base, None
+                    entry = bucket[kind * 96 + i]
+                    item = entry >> 24
+                    row = (entry >> 16) & 255
+                    base = entry & 0xFFFF
+                    best = None
                     for c in range(CHOICES[hops]):
-                        _, ends, words = chain(base + 4 * c, hops)
-                        cost = (ends[-1] << 16) + words
+                        links = tab[base + c]
+                        seen, words, ends = 0, 0, 0
+                        for h in range(hops):
+                            word = occ[(links >> (8 * h)) & 255]
+                            used = word | seen
+                            seen = used ^ (used + 1)
+                            words = words + word
+                            ends = ends + (seen << (8 * h))
+                        cost = (seen << 16) + words
                         if best is None:
-                            best = cost
+                            best, best_links, best_ends = cost, links, ends
                         else:
-                            best_at = jnp.where(cost < best, base + 4 * c, best_at)
-                            best = jnp.minimum(cost, best)
-                    fits = best < jnp.where(jk < 3, 1 << (16 + SLOTS_FIRST), 1 << (16 + SLOTS))
-
-                    @pl.when(fits)
-                    def _():
-                        links, ends, _ = chain(best_at, hops)
-                        source = block >> 4
-                        for link, end in zip(links, ends):
-                            occ[link] = (occ[link] | ((end + 1) >> 1)) + LOAD
-                            slot = tab[SLOT_AT + end]
-                            tbl[link * 8 + slot] = source
-                            source = ROWS_KV + 4 * slot + (link & 3)
-                        posn[item] = source
-
-                    @pl.when(jnp.logical_not(fits))
-                    def _():
-                        front[item] = 1
-
-                    return missed + jnp.where(fits, 0, 1)
+                            less = cost < best
+                            best = jnp.where(less, cost, best)
+                            best_links = jnp.where(less, links, best_links)
+                            best_ends = jnp.where(less, ends, best_ends)
+                    fits = best < jnp.where((item & 7) < 3, 1 << (16 + SLOTS_FIRST), 1 << (16 + SLOTS))
+                    source = row
+                    load = LOAD if hops > 1 else 0
+                    for h in range(hops):
+                        link = (best_links >> (8 * h)) & 255
+                        end = (best_ends >> (8 * h)) & 255
+                        occ[link] = occ[link] + jnp.where(fits, ((end + 1) >> 1) + load, 0)
+                        slot = tab[SLOT_AT + end]
+                        tbl[jnp.where(fits, link * 8 + slot, NODES * 4 * 8)] = source
+                        source = ROWS_KV + 4 * slot + (link & 3)
+                    posn[item] = jnp.where(fits, source, row)
+                    late = jnp.where(fits, 0, 1)
+                    front[item] = front[item] | late
+                    return missed + late
 
                 missed = lax.fori_loop(0, cnt[kind], route, missed)
             return missed
@@ -294,13 +287,13 @@
         for d in range(4):
             send[t * 4 + d] = tbl[(me * 4 + d) * 8 + t]
     for jk in range(6):
-        block = lists[me, 0, 64 + jk]
+        block = rows[me, 0, 64 + jk].astype(jnp.int32)
         owner = block & (NODES - 1)
         row = block >> 4
         place[jk] = posn[me * 8 + jk]
         limit[jk] = start[0] - block * BLK
-        factor[jk] = scales[owner, 0, row] * (LOG2E / math.sqrt(DH))
-        factor[8 + jk] = scales[owner, 0, ROWS_KV + row]
+        factor[jk] = rows[owner, 0, row] * (LOG2E / math.sqrt(DH))
+        factor[8 + jk] = rows[owner, 0, ROWS_KV + row]
     flag[...] = jnp.full((1, 128), missed, jnp.int32).astype(jnp.float32)
 
 
@@ -408,7 +401,7 @@
                 kv_copy(t, d, h).start()
 
     def rows_of(c):
-        return pl.ds(pl.multiple_of(c * QROWS, QROWS), QROWS)
+        return pl.ds(pl.multiple_of(c * CROWS, CROWS), CROWS)
 
     def load_q(j, c):
         tile = qb[j, rows_of(c), :]
@@ -424,7 +417,7 @@
 
     def own_tile(j, c):
         scores = scores_of(load_q(j, c), sk[j]) * (LOG2E / math.sqrt(DH))
-        row = lax.broadcasted_iota(jnp.int32, (TILE_ROWS, 1), 0) % QROWS + c * QROWS
+        row = lax.broadcasted_iota(jnp.int32, (TILE_ROWS, 1), 0) % CROWS + c * CROWS
         scores = jnp.where(column <= row, scores, NEG)
         high = jnp.max(scores, axis=1, keepdims=True)
         weights = jnp.exp2(scores - high).astype(jnp.bfloat16)
@@ -458,24 +451,27 @@
             total = total + more[:, DH:]
         done = (summed / total).astype(jnp.bfloat16)
         for h in range(HG):
-            ob[j, rows_of(c), h * DH : (h + 1) * DH] = done[h * QROWS : (h + 1) * QROWS]
+            ob[j, rows_of(c), h * DH : (h + 1) * DH] = done[h * CROWS : (h + 1) * CROWS]
 
     def own_block(j):
         def step(c, _):
             own_tile(j, c)
             return 0
 
-        lax.fori_loop(0, PEERS, step, 0)
-
-    def cache_blocks(j):
-        def step(k, _):
-            cache_tile(j, peer(k))
-            o_copy(j, k).start()
+        lax.fori_loop(0, CHIPS, step, 0)
+
+    def cache_blocks(j, begin, end):
+        def step(pair, _):
+            cache_tile(j, peer(2 * pair) // 2)
+            o_copy(j, 2 * pair).start()
+            o_copy(j, 2 * pair + 1).start()
             return 0
 
-        lax.fori_loop(0, PEERS - 1, step, 0)
-        cache_tile(j, r)
-        o_own(j).start()
+        lax.fori_loop(begin, min(end, CHIPS - 1), step, 0)
+        if end == CHIPS:
+            cache_tile(j, y)
+            o_copy(j, PEERS - 2).start()
+            o_own(j).start()
 
     for k in range(PEERS - 1):
         q_copy(k).start()
@@ -498,8 +494,12 @@
             if (t, h) == (4, 0):
                 own_block(1)
             if (t, h) == (SLOTS_FIRST, 1):
-                cache_blocks(0)
-    cache_blocks(1)
+                cache_blocks(0, 0, 2)
+            if (t, h) == (SLOTS_FIRST + 1, 0):
+                cache_blocks(0, 2, 3)
+            if (t, h) == (SLOTS_FIRST + 1, 1):
+                cache_blocks(0, 3, CHIPS)
+    cache_blocks(1, 0, CHIPS)
     for k in range(PEERS - 1):
         f_copy(k).wait()
     worst = flags[0]
@@ -516,6 +516,26 @@
             o_copy(j, k).wait()
 
 
+def copy_kernel(x, out, sem):
+    copies = [pltpu.make_async_copy(x.at[j], out.at[j], sem.at[j]) for j in range(2)]
+    for copy in copies:
+        copy.start()
+    for copy in copies:
+        copy.wait()
+
+
+def settle(attended):
+    hbm = pl.BlockSpec(memory_space=pl.ANY)
+    return pl.pallas_call(
+        copy_kernel,
+        out_shape=jax.ShapeDtypeStruct(attended.shape, attended.dtype),
+        in_specs=[hbm],
+        out_specs=hbm,
+        scratch_shapes=[pltpu.SemaphoreType.DMA((2,))],
+        name="settle",
+    )(attended)
+
+
 def per_device(
     queries, span_keys, span_values, cache_keys, cache_values, key_scales, value_scales, selections, start
 ):
@@ -524,14 +544,11 @@
     vmem = pl.BlockSpec(memory_space=pltpu.VMEM)
     hbm = pl.BlockSpec(memory_space=pl.ANY)
     dma = pltpu.SemaphoreType.DMA
-    scales, lists = pl.pallas_call(
+    rows = pl.pallas_call(
         lists_kernel,
-        out_shape=(
-            jax.ShapeDtypeStruct((NODES, 1, 128), f32),
-            jax.ShapeDtypeStruct((NODES, 1, 128), i32),
-        ),
+        out_shape=jax.ShapeDtypeStruct((NODES, 1, 128), f32),
         in_specs=[vmem] * 3,
-        out_specs=(vmem, vmem),
+        out_specs=vmem,
         scratch_shapes=[
             pltpu.VMEM((1, 128), f32),
             pltpu.VMEM((NODES, 1, 128), f32),
@@ -550,18 +567,18 @@
             jax.ShapeDtypeStruct((16,), f32),
             jax.ShapeDtypeStruct((1, 128), f32),
         ),
-        in_specs=[smem] * 4,
+        in_specs=[smem] * 3,
         out_specs=(smem, smem, smem, smem, vmem),
         scratch_shapes=[
-            pltpu.SMEM((NODES * 4,), i32),
+            pltpu.SMEM((NODES * 4 + 8,), i32),
             pltpu.SMEM((13 * 96,), i32),
             pltpu.SMEM((16,), i32),
-            pltpu.SMEM((NODES * 4 * 8,), i32),
+            pltpu.SMEM((NODES * 4 * 8 + 8,), i32),
             pltpu.SMEM((NODES * 8,), i32),
             pltpu.SMEM((NODES * 8,), i32),
         ],
         name="plan",
-    )(lists, scales, start, jnp.asarray(TABLES))
+    )(rows, start, jnp.asarray(TABLES))
     attended, over = pl.pallas_call(
         main_kernel,
         out_shape=(
@@ -579,8 +596,8 @@
             pltpu.VMEM((2, BLK, WIDE), bf16),
             pltpu.VMEM((2, BLK, DH), bf16),
             pltpu.VMEM((2, BLK, DH), bf16),
-            pltpu.VMEM((2, PEERS, TILE_ROWS, 2 * DH), f32),
-            pltpu.VMEM((2, PEERS, TILE_ROWS, DH), f32),
+            pltpu.VMEM((2, CHIPS, TILE_ROWS, 2 * DH), f32),
+            pltpu.VMEM((2, CHIPS, TILE_ROWS, DH), f32),
             pltpu.VMEM((PEERS, 1, 128), f32),
             dma((8,)),
             dma((SLOTS, 4, 2)),
@@ -599,8 +616,8 @@
     )(send, place, limit, factor, flag, queries, span_keys, span_values, cache_keys, cache_values)
     return lax.cond(
         over[0, 0] > 0,
-        lambda: padded(queries, span_keys, span_values, cache_keys, cache_values, start, lists, scales),
-        lambda: attended,
+        lambda: padded(queries, span_keys, span_values, cache_keys, cache_values, start, rows),
+        lambda: settle(attended),
     )
 
 

time: 89.6 us -> 76.5 us (0.85)
  Pallas kernels: 85.2 us -> 74 us
  local copies, waits for them, and re-layouts: 2.29 us -> 0.97 us
    pallas_call x1, Pallas kernels: 65.5 us -> 55.4 us  [per_device(): pl.pallas_call(main_kernel, out_shape=(jax.ShapeDtypeStruct(queries.shape...]
    unnamed x3 -> x4, local copies, waits for them, and re-layouts: 2.29 us -> 0.97 us
    pallas_call x1, Pallas kernels: 8.79 us -> 7.66 us  [per_device(): pl.pallas_call(plan_kernel, out_shape=(jax.ShapeDtypeStruct((4 * SLOTS,),...]
    pallas_call x1 -> x2, Pallas kernels: 10.8 us -> 10.9 us  [the longest x1 10.8 us: per_device(): pl.pallas_call(lists_kernel, out_shape=jax.ShapeDtypeStruct((NODES, 1, 12...]
where the time goes in v3:
time: 76.5 us; the launch traced here: 76.3 us
  Pallas kernels  74 us (97%)
  between operations  1.32 us (2%)
  local copies, waits for them, and re-layouts  0.97 us (1%)
    pallas_call x1, Pallas kernels, per_device(): pl.pallas_call(main_kernel, out_shape=(jax.ShapeDtypeStruct(queries.shape...  55.4 us
    pallas_call x1, Pallas kernels, per_device(): pl.pallas_call(lists_kernel, out_shape=jax.ShapeDtypeStruct((NODES, 1, 12...  10.8 us
    pallas_call x1, Pallas kernels, per_device(): pl.pallas_call(plan_kernel, out_shape=(jax.ShapeDtypeStruct((4 * SLOTS,),...  7.66 us

profile of v3, /device:TPU:1, one launch (start us, length us, event | category | flops | bytes accessed | tf_op | source)
XLA Modules:
  0.0 76.3 jit_solution(785195045663485892)
XLA Ops:
  0.0 10.8 %lists.1.rows = f32[16,1,128]{2,1,0:T(1,128)S(1)} custom-call(bf16[1,32]{1,0:T(2,128)(2,1)} %bitcast.171, bf16[1,32]{1,0:T(2,128)(2,1)} %bitcast.172, s32[2,3]{1,0:T(2,128)} %bitcast.170), custom_call_target="tpu_custom_call" | custom-call | tf_op jit(solution)/shard_map/lists/pallas_call | solution.py:547
  11.5 7.7 %plan.1 = (s32[24]{0:T(128)}, s32[8]{0:T(128)}, s32[8]{0:T(128)}, f32[16]{0:T(128)}, f32[1,128]{1,0:T(1,128)}) custom-call(f32[16,1,128]{2,1,0:T(1,128)S(1)} %lists.1.rows, s32[1]{0:T(128)S(6)} %copy.149.start, s32[2048]{0:T(1024)} %constant.114.clone.tab), custom_call_target="tpu_custom_call" | custom-call | tf_op jit(solution)/shard_map/plan/pallas_call | solution.py:561
  19.2 0.0 copy-start.1
  19.2 55.4 %exchange_attend.1 = (bf16[2,1,64,4096]{3,2,1,0:T(8,128)(2,1)S(1)}, f32[1,128]{1,0:T(1,128)}) custom-call(s32[24]{0:T(128)} %get-tuple-element.94.send, s32[8]{0:T(128)} %get-tuple-element.95.place, s32[8]{0:T(128)} %get-tuple-element.96.limit, f32[16]{0:T(128)} %get-tuple-element.97.factor, f32[1,128]{1,0:T(1,128)} %get-tuple-element.98.flag, ...), custom_call_target="tpu_custom_call" | custom-call | tf_op jit(solution)/shard_map/exchange_attend/pallas_call | solution.py:582
  75.2 0.0 copy-done.1
  75.2 0.1 conditional.1
  75.2 0.1 settle.1
  75.3 0.0 copy-start.2
  75.3 1.0 %copy-done.2 = bf16[2,1,64,4096]{3,2,0,1:T(8,128)(2,1)} copy-done((bf16[2,1,64,4096]{3,2,0,1:T(8,128)(2,1)}, bf16[2,1,64,4096]{3,2,0,1:T(8,128)(2,1)S(1)}, u32[]{:S(2)}) %copy-start.2) | copy-done | bytes 1048600
Async XLA Ops:
  19.2 56.0 %copy-start.1 = (bf16[2,1,64,4096]{3,2,1,0:T(8,128)(2,1)S(1)}, bf16[2,1,64,4096]{3,2,1,0:T(8,128)(2,1)}, u32[]{:S(2)}) copy-start(bf16[2,1,64,4096]{3,2,1,0:T(8,128)(2,1)} %q.1) | copy-start | bytes 3145732
  75.3 1.0 %copy-start.2 = (bf16[2,1,64,4096]{3,2,0,1:T(8,128)(2,1)}, bf16[2,1,64,4096]{3,2,0,1:T(8,128)(2,1)S(1)}, u32[]{:S(2)}) copy-start(bf16[2,1,64,4096]{3,2,0,1:T(8,128)(2,1)S(1)} %get-tuple-element.101) | copy-start | bytes 3145732

commit v4 on v3

--- a/solution.py
+++ b/solution.py
@@ -23,9 +23,7 @@
 PEERS = 8
 QROWS = BLK // PEERS
 WIDE = HG * DH
-CHIPS = PEERS // 2
-CROWS = 2 * QROWS
-TILE_ROWS = HG * CROWS
+TILE_ROWS = HG * QROWS
 POOL = ROWS_KV + 4 * SLOTS
 LOG2E = 1.4426950408889634
 NEG = -1e30
@@ -232,19 +230,24 @@
         for kind in range(13):
             cnt[kind] = 0
         lax.fori_loop(0, NODES, sort_dest, 0)
+        for kind in range(12):
+            bucket[kind * 96 + cnt[kind]] = 0
 
         def run_phase(phase, missed):
             for hops in (4, 3, 2, 1):
                 kind = phase * 4 + 4 - hops
 
-                def route(i, missed, kind=kind, hops=hops):
+                def fetch(i, kind=kind, hops=hops):
                     entry = bucket[kind * 96 + i]
+                    return (entry,) + tuple(tab[(entry & 0xFFFF) + c] for c in range(CHOICES[hops]))
+
+                def route(i, carry, hops=hops, fetch=fetch):
+                    missed, entry = carry[:2]
+                    upcoming = fetch(i + 1)
                     item = entry >> 24
                     row = (entry >> 16) & 255
-                    base = entry & 0xFFFF
                     best = None
-                    for c in range(CHOICES[hops]):
-                        links = tab[base + c]
+                    for links in carry[2:]:
                         seen, words, ends = 0, 0, 0
                         for h in range(hops):
                             word = occ[(links >> (8 * h)) & 255]
@@ -273,9 +276,9 @@
                     posn[item] = jnp.where(fits, source, row)
                     late = jnp.where(fits, 0, 1)
                     front[item] = front[item] | late
-                    return missed + late
-
-                missed = lax.fori_loop(0, cnt[kind], route, missed)
+                    return (missed + late,) + upcoming
+
+                missed = lax.fori_loop(0, cnt[kind], route, (missed,) + fetch(0))[0]
             return missed
 
         return lax.fori_loop(0, 3, run_phase, jnp.int32(0)), carry[1] + 1
@@ -300,7 +303,7 @@
 def main_kernel(
     send, place, limit, factor, flag, q, sk_hbm, sv_hbm, ck_hbm, cv_hbm,
     out, over,
-    kp, vp, snd, rcv, qb, ob, sk, sv, acc, top, flags,
+    kp, vp, snd, rcv, qb, ob, sk, sv, acc, top, even, odd, even_top, odd_top, flags,
     load_sem, kv_send, kv_recv, q_send, q_recv, o_send, o_recv, f_send, f_recv,
 ):
     s, r = lax.axis_index("seq"), lax.axis_index("inter")
@@ -401,7 +404,7 @@
                 kv_copy(t, d, h).start()
 
     def rows_of(c):
-        return pl.ds(pl.multiple_of(c * CROWS, CROWS), CROWS)
+        return pl.ds(pl.multiple_of(c * QROWS, QROWS), QROWS)
 
     def load_q(j, c):
         tile = qb[j, rows_of(c), :]
@@ -417,7 +420,7 @@
 
     def own_tile(j, c):
         scores = scores_of(load_q(j, c), sk[j]) * (LOG2E / math.sqrt(DH))
-        row = lax.broadcasted_iota(jnp.int32, (TILE_ROWS, 1), 0) % CROWS + c * CROWS
+        row = lax.broadcasted_iota(jnp.int32, (TILE_ROWS, 1), 0) % QROWS + c * QROWS
         scores = jnp.where(column <= row, scores, NEG)
         high = jnp.max(scores, axis=1, keepdims=True)
         weights = jnp.exp2(scores - high).astype(jnp.bfloat16)
@@ -426,51 +429,62 @@
         )
         top[j, c] = jnp.broadcast_to(high, (TILE_ROWS, DH))
 
-    def cache_tile(j, c):
+    def score(j, k, held, held_top):
+        c = peer(k)
         query = load_q(j, c)
-        before = top[j, c][:, :1]
-        parts = []
-        high = before
-        for i in range(3 * j, 3 * j + 3):
-            bias = jnp.where(column < limit[i], 0.0, NEG)
-            part = scores_of(query, kp[place[i]]) * factor[i] + bias
+        high = top[j, c][:, :1]
+        for i in range(3):
+            bias = jnp.where(column < limit[3 * j + i], 0.0, NEG)
+            part = scores_of(query, kp[place[3 * j + i]]) * factor[3 * j + i] + bias
             high = jnp.maximum(high, jnp.max(part, axis=1, keepdims=True))
-            parts.append(part)
-        fade = jnp.exp2(before - high)
+            held[i] = part
+        held_top[...] = jnp.broadcast_to(high, (TILE_ROWS, DH))
+
+    def attend_tile(j, k, held, held_top):
+        c = peer(k)
+        high = held_top[...]
+        fade = jnp.exp2(top[j, c] - high)
         old = acc[j, c]
         summed = old[:, :DH] * fade
         total = old[:, DH:] * fade
-        for i, part in zip(range(3 * j, 3 * j + 3), parts):
-            weights = jnp.exp2(part - high).astype(jnp.bfloat16)
+        for i in range(3):
+            weights = jnp.exp2(held[i] - high[:, :1]).astype(jnp.bfloat16)
             more = jnp.dot(
                 weights,
-                jnp.concatenate([vp[place[i]], ones], axis=1),
+                jnp.concatenate([vp[place[3 * j + i]], ones], axis=1),
                 preferred_element_type=jnp.float32,
             )
-            summed = summed + more[:, :DH] * factor[8 + i]
+            summed = summed + more[:, :DH] * factor[8 + 3 * j + i]
             total = total + more[:, DH:]
         done = (summed / total).astype(jnp.bfloat16)
         for h in range(HG):
-            ob[j, rows_of(c), h * DH : (h + 1) * DH] = done[h * CROWS : (h + 1) * CROWS]
+            ob[j, rows_of(c), h * DH : (h + 1) * DH] = done[h * QROWS : (h + 1) * QROWS]
 
     def own_block(j):
         def step(c, _):
             own_tile(j, c)
             return 0
 
-        lax.fori_loop(0, CHIPS, step, 0)
+        lax.fori_loop(0, PEERS, step, 0)
 
     def cache_blocks(j, begin, end):
         def step(pair, _):
-            cache_tile(j, peer(2 * pair) // 2)
+            score(j, 2 * pair + 1, odd, odd_top)
+            attend_tile(j, 2 * pair, even, even_top)
             o_copy(j, 2 * pair).start()
+            score(j, 2 * pair + 2, even, even_top)
+            attend_tile(j, 2 * pair + 1, odd, odd_top)
             o_copy(j, 2 * pair + 1).start()
             return 0
 
-        lax.fori_loop(begin, min(end, CHIPS - 1), step, 0)
-        if end == CHIPS:
-            cache_tile(j, y)
+        if begin == 0:
+            score(j, 0, even, even_top)
+        lax.fori_loop(begin // 2, min(end, PEERS - 2) // 2, step, 0)
+        if end == PEERS:
+            score(j, PEERS - 1, odd, odd_top)
+            attend_tile(j, PEERS - 2, even, even_top)
             o_copy(j, PEERS - 2).start()
+            attend_tile(j, PEERS - 1, odd, odd_top)
             o_own(j).start()
 
     for k in range(PEERS - 1):
@@ -496,10 +510,10 @@
             if (t, h) == (SLOTS_FIRST, 1):
                 cache_blocks(0, 0, 2)
             if (t, h) == (SLOTS_FIRST + 1, 0):
-                cache_blocks(0, 2, 3)
+                cache_blocks(0, 2, 4)
             if (t, h) == (SLOTS_FIRST + 1, 1):
-                cache_blocks(0, 3, CHIPS)
-    cache_blocks(1, 0, CHIPS)
+                cache_blocks(0, 4, PEERS)
+    cache_blocks(1, 0, PEERS)
     for k in range(PEERS - 1):
         f_copy(k).wait()
     worst = flags[0]
@@ -571,7 +585,7 @@
         out_specs=(smem, smem, smem, smem, vmem),
         scratch_shapes=[
             pltpu.SMEM((NODES * 4 + 8,), i32),
-            pltpu.SMEM((13 * 96,), i32),
+            pltpu.SMEM((13 * 96 + 8,), i32),
             pltpu.SMEM((16,), i32),
             pltpu.SMEM((NODES * 4 * 8 + 8,), i32),
             pltpu.SMEM((NODES * 8,), i32),
@@ -596,8 +610,12 @@
             pltpu.VMEM((2, BLK, WIDE), bf16),
             pltpu.VMEM((2, BLK, DH), bf16),
             pltpu.VMEM((2, BLK, DH), bf16),
-            pltpu.VMEM((2, CHIPS, TILE_ROWS, 2 * DH), f32),
-            pltpu.VMEM((2, CHIPS, TILE_ROWS, DH), f32),
+            pltpu.VMEM((2, PEERS, TILE_ROWS, 2 * DH), f32),
+            pltpu.VMEM((2, PEERS, TILE_ROWS, DH), f32),
+            pltpu.VMEM((3, TILE_ROWS, BLK), f32),
+            pltpu.VMEM((3, TILE_ROWS, BLK), f32),
+            pltpu.VMEM((TILE_ROWS, DH), f32),
+            pltpu.VMEM((TILE_ROWS, DH), f32),
             pltpu.VMEM((PEERS, 1, 128), f32),
             dma((8,)),
             dma((SLOTS, 4, 2)),

time: 76.5 us -> 73.9 us (0.966)
  Pallas kernels: 74 us -> 71.1 us
    pallas_call x1, Pallas kernels: 55.4 us -> 53.5 us  [per_device(): pl.pallas_call(main_kernel, out_shape=(jax.ShapeDtypeStruct(queries.shape...]
    pallas_call x1, Pallas kernels: 7.66 us -> 6.65 us  [per_device(): pl.pallas_call(plan_kernel, out_shape=(jax.ShapeDtypeStruct((4 * SLOTS,),...]
where the time goes in v4:
time: 73.9 us; the launch traced here: 73.6 us
  Pallas kernels  71.1 us (96%)
  between operations  1.32 us (2%)
  local copies, waits for them, and re-layouts  0.97 us (1%)
    pallas_call x1, Pallas kernels, per_device(): pl.pallas_call(main_kernel, out_shape=(jax.ShapeDtypeStruct(queries.shape...  53.5 us
    pallas_call x1, Pallas kernels, per_device(): pl.pallas_call(lists_kernel, out_shape=jax.ShapeDtypeStruct((NODES, 1, 12...  10.8 us
    pallas_call x1, Pallas kernels, per_device(): pl.pallas_call(plan_kernel, out_shape=(jax.ShapeDtypeStruct((4 * SLOTS,),...  6.65 us

profile of v4, /device:TPU:1, one launch (start us, length us, event | category | flops | bytes accessed | tf_op | source)
XLA Modules:
  0.0 73.6 jit_solution(17587741328987359405)
XLA Ops:
  0.0 10.8 %lists.1.rows = f32[16,1,128]{2,1,0:T(1,128)S(1)} custom-call(bf16[1,32]{1,0:T(2,128)(2,1)} %bitcast.171, bf16[1,32]{1,0:T(2,128)(2,1)} %bitcast.172, s32[2,3]{1,0:T(2,128)} %bitcast.170), custom_call_target="tpu_custom_call" | custom-call | tf_op jit(solution)/shard_map/lists/pallas_call | solution.py:561
  11.5 6.6 %plan.1 = (s32[24]{0:T(128)}, s32[8]{0:T(128)}, s32[8]{0:T(128)}, f32[16]{0:T(128)}, f32[1,128]{1,0:T(1,128)}) custom-call(f32[16,1,128]{2,1,0:T(1,128)S(1)} %lists.1.rows, s32[1]{0:T(128)S(6)} %copy.149.start, s32[2048]{0:T(1024)} %constant.114.clone.tab), custom_call_target="tpu_custom_call" | custom-call | tf_op jit(solution)/shard_map/plan/pallas_call | solution.py:575
  18.1 0.0 copy-start.1
  18.2 53.5 %exchange_attend.1 = (bf16[2,1,64,4096]{3,2,1,0:T(8,128)(2,1)S(1)}, f32[1,128]{1,0:T(1,128)}) custom-call(s32[24]{0:T(128)} %get-tuple-element.94.send, s32[8]{0:T(128)} %get-tuple-element.95.place, s32[8]{0:T(128)} %get-tuple-element.96.limit, f32[16]{0:T(128)} %get-tuple-element.97.factor, f32[1,128]{1,0:T(1,128)} %get-tuple-element.98.flag, ...), custom_call_target="tpu_custom_call" | custom-call | tf_op jit(solution)/shard_map/exchange_attend/pallas_call | solution.py:596
  72.3 0.0 copy-done.1
  72.3 0.3 conditional.1
  72.3 0.1 settle.1
  72.6 0.0 copy-start.2
  72.6 1.0 %copy-done.2 = bf16[2,1,64,4096]{3,2,0,1:T(8,128)(2,1)} copy-done((bf16[2,1,64,4096]{3,2,0,1:T(8,128)(2,1)}, bf16[2,1,64,4096]{3,2,0,1:T(8,128)(2,1)S(1)}, u32[]{:S(2)}) %copy-start.2) | copy-done | bytes 1048600
Async XLA Ops:
  18.1 54.1 %copy-start.1 = (bf16[2,1,64,4096]{3,2,1,0:T(8,128)(2,1)S(1)}, bf16[2,1,64,4096]{3,2,1,0:T(8,128)(2,1)}, u32[]{:S(2)}) copy-start(bf16[2,1,64,4096]{3,2,1,0:T(8,128)(2,1)} %q.1) | copy-start | bytes 3145732
  72.6 1.0 %copy-start.2 = (bf16[2,1,64,4096]{3,2,0,1:T(8,128)(2,1)}, bf16[2,1,64,4096]{3,2,0,1:T(8,128)(2,1)S(1)}, u32[]{:S(2)}) copy-start(bf16[2,1,64,4096]{3,2,0,1:T(8,128)(2,1)S(1)} %get-tuple-element.101) | copy-start | bytes 3145732
